TPU v7x, 256 devices: a whole 4x4x8 slice. The times are simulated.
256 devices in a mesh: dp: 64 (over z, y_lo, x), lat: 4 (over y_hi, core).
Axes of the slice: x: 4, y: 4 (y_hi: 2, y_lo: 2; y = y_hi * 2 + y_lo), z: 8, core: 2. Of those that a mesh axis runs over, the one named last changes fastest.
Arguments:
- tokens: bfloat16 [196608, 512], P(('dp', 'lat')), may hold values from -6 to 6
- latents: bfloat16 [12288, 1024], P(('dp', 'lat')), may hold values from -6 to 6
- gain_self: float32 [512], replicated, may hold values from 0.1 to 1.9
- w_qkv_tok: bfloat16 [512, 1536], replicated, may hold values from -1 to 1
- w_o_tok: bfloat16 [512, 512], replicated, may hold values from -0.25 to 0.25
- gain_read: float32 [512], replicated, may hold values from 0.1 to 1.9
- w_kv_read: bfloat16 [512, 2048], replicated, may hold values from -1 to 1
- gain_lat: float32 [1024], replicated, may hold values from 0.1 to 1.9
- w_q_read: bfloat16 [1024, 1024], replicated, may hold values from -1 to 1
- gain_glob: float32 [1024], replicated, may hold values from 0.1 to 1.9
- w_qkv_glob: bfloat16 [3, 1024, 1024], P(None, None, 'lat'), may hold values from -1 to 1
- w_o_glob: bfloat16 [1024, 1024], P('lat'), may hold values from -0.375 to 0.375
- gain_write: float32 [512], replicated, may hold values from 0.1 to 1.9
- w_q_write: bfloat16 [512, 512], replicated, may hold values from -1 to 1
- gain_wlat: float32 [1024], replicated, may hold values from 0.1 to 1.9
- w_kv_write: bfloat16 [1024, 1024], replicated, may hold values from -1 to 1
Outputs:
- tokens_out: bfloat16 [196608, 512], P(('dp', 'lat'))
- latents_out: bfloat16 [12288, 1024], P(('dp', 'lat'))
All inputs are finite; a program needn't handle non-finite values.
Results may differ from a plain program's by a relative error of at most 0.015.
Values may be sent and summed in bfloat16 or wider, within the bound.
No kernel may reach another device: no remote copies, remote signals or barrier semaphores. Data moves between devices by JAX's collectives and lax.ppermute only.
A program may use at most 128 MiB of HBM per device.

v0:
```python
import jax
import jax.numpy as jnp
from jax import lax
from jax.sharding import PartitionSpec as P

HEAD = 64
G = 256
NLAT = 16


def rms_norm(values, gain):
    floats = values.astype(jnp.float32)
    factor = lax.rsqrt(jnp.mean(floats * floats, axis=-1, keepdims=True) + 1e-06)
    return (floats * factor * gain).astype(jnp.bfloat16)


def attend(query, keys, values):
    scores = jnp.einsum("qhe,khe->hqk", query, keys, preferred_element_type=jnp.float32) * HEAD ** (
        -0.5
    )
    peak = jnp.max(scores, axis=-1, keepdims=True)
    weights = jnp.exp(scores - peak)
    total = jnp.sum(weights, axis=-1)
    mixed = jnp.einsum(
        "hqk,khe->hqe", weights.astype(jnp.bfloat16), values, preferred_element_type=jnp.float32
    )
    return jnp.transpose(mixed / total[:, :, None], (1, 0, 2))


def front(group, lat_rows, gain_self, w_qkv_tok, w_o_tok, gain_read, w_kv_read, gain_lat, w_q_read):
    rows = group.shape[0]
    packed = jnp.dot(rms_norm(group, gain_self), w_qkv_tok, preferred_element_type=jnp.float32)
    packed = packed.astype(jnp.bfloat16).reshape(rows, 3, -1, HEAD)
    mixed = attend(packed[:, 0], packed[:, 1], packed[:, 2]).reshape(rows, -1).astype(jnp.bfloat16)
    tokens_mid = (
        group.astype(jnp.float32) + jnp.dot(mixed, w_o_tok, preferred_element_type=jnp.float32)
    ).astype(jnp.bfloat16)
    key_vals = jnp.dot(
        rms_norm(tokens_mid, gain_read), w_kv_read, preferred_element_type=jnp.float32
    )
    key_vals = key_vals.astype(jnp.bfloat16).reshape(rows, 2, -1, HEAD)
    query = jnp.dot(rms_norm(lat_rows, gain_lat), w_q_read, preferred_element_type=jnp.float32)
    query = query.astype(jnp.bfloat16).reshape(lat_rows.shape[0], -1, HEAD)
    read = attend(query, key_vals[:, 0], key_vals[:, 1]).reshape(lat_rows.shape[0], -1)
    return (tokens_mid, (lat_rows.astype(jnp.float32) + read).astype(jnp.bfloat16))


def back(tokens_mid, lat_rows, gain_write, w_q_write, gain_wlat, w_kv_write):
    rows = tokens_mid.shape[0]
    query = jnp.dot(rms_norm(tokens_mid, gain_write), w_q_write, preferred_element_type=jnp.float32)
    query = query.astype(jnp.bfloat16).reshape(rows, -1, HEAD)
    key_vals = jnp.dot(
        rms_norm(lat_rows, gain_wlat), w_kv_write, preferred_element_type=jnp.float32
    )
    key_vals = key_vals.astype(jnp.bfloat16).reshape(lat_rows.shape[0], 2, -1, HEAD)
    written = attend(query, key_vals[:, 0], key_vals[:, 1]).reshape(rows, -1)
    return (tokens_mid.astype(jnp.float32) + written).astype(jnp.bfloat16)


def fold_update(carry, query, keys, values):
    row_max, row_total, accum = carry
    scores = jnp.einsum("qhe,khe->hqk", query, keys, preferred_element_type=jnp.float32) * HEAD ** (
        -0.5
    )
    new_max = jnp.maximum(row_max, jnp.max(scores, axis=-1))
    weights = jnp.exp(scores - new_max[:, :, None])
    row_total = jnp.sum(weights, axis=-1)
    accum = jnp.einsum(
        "hqk,khe->hqe", weights.astype(jnp.bfloat16), values, preferred_element_type=jnp.float32
    )
    return (new_max, row_total, accum)


def local(
    tokens,
    latents,
    gain_self,
    w_qkv_tok,
    w_o_tok,
    gain_read,
    w_kv_read,
    gain_lat,
    w_q_read,
    gain_glob,
    w_qkv_glob,
    w_o_glob,
    gain_write,
    w_q_write,
    gain_wlat,
    w_kv_write,
):
    width = tokens.shape[1]
    lat_width = latents.shape[1]
    groups = tokens.reshape(-1, G, width)
    lat_groups = latents.reshape(-1, NLAT, lat_width)
    tokens_mid, latents_mid = jax.vmap(
        lambda group, lat_rows: front(
            group, lat_rows, gain_self, w_qkv_tok, w_o_tok, gain_read, w_kv_read, gain_lat, w_q_read
        )
    )(groups, lat_groups)
    latents_mid = latents_mid.reshape(-1, lat_width)
    normed = rms_norm(latents_mid, gain_glob)
    block = lax.all_gather(normed, "lat", axis=0, tiled=True)
    block_rows = block.shape[0]
    heads_here = w_qkv_glob.shape[2] // HEAD
    query = (
        jnp.dot(block, w_qkv_glob[0], preferred_element_type=jnp.float32)
        .astype(jnp.bfloat16)
        .reshape(block_rows, heads_here, HEAD)
    )
    start_carry = (
        jnp.full((heads_here, block_rows), -1e30, jnp.float32),
        jnp.zeros((heads_here, block_rows), jnp.float32),
        jnp.zeros((heads_here, block_rows, HEAD), jnp.float32),
    )
    keys_here = jnp.dot(block, w_qkv_glob[1], preferred_element_type=jnp.float32).astype(
        jnp.bfloat16
    )
    values_here = jnp.dot(block, w_qkv_glob[2], preferred_element_type=jnp.float32).astype(
        jnp.bfloat16
    )
    keys = lax.all_gather(keys_here, "dp", axis=0, tiled=True)
    values = lax.all_gather(values_here, "dp", axis=0, tiled=True)
    piece_rows = keys.shape[0]
    carry = fold_update(
        start_carry,
        query,
        keys.reshape(piece_rows, heads_here, HEAD),
        values.reshape(piece_rows, heads_here, HEAD),
    )
    mixed = (carry[2] / carry[1][:, :, None]).astype(jnp.bfloat16)
    mixed = jnp.transpose(mixed, (1, 0, 2)).reshape(block_rows, heads_here * HEAD)
    summed = lax.psum_scatter(
        jnp.dot(mixed, w_o_glob, preferred_element_type=jnp.float32).astype(jnp.bfloat16),
        "lat",
        scatter_dimension=0,
        tiled=True,
    ).astype(jnp.float32)
    latents_out = (latents_mid.astype(jnp.float32) + summed).astype(jnp.bfloat16)
    tokens_out = jax.vmap(
        lambda tok_rows, lat_rows: back(
            tok_rows, lat_rows, gain_write, w_q_write, gain_wlat, w_kv_write
        )
    )(tokens_mid, latents_out.reshape(-1, NLAT, lat_width))
    return (tokens_out.reshape(-1, width), latents_out)


def solution(mesh):
    placed = (
        P(("dp", "lat"), None),
        P(("dp", "lat"), None),
        P(),
        P(),
        P(),
        P(),
        P(),
        P(),
        P(),
        P(),
        P(None, None, "lat"),
        P("lat", None),
        P(),
        P(),
        P(),
        P(),
    )
    return jax.shard_map(
        local,
        mesh=mesh,
        in_specs=placed,
        out_specs=(P(("dp", "lat"), None), P(("dp", "lat"), None)),
        check_vma=False,
    )
```

profile of v0, /device:TPU:1, one launch (start us, length us, event | category | flops | bytes accessed | tf_op | source)
XLA Modules:
  0.0 740.2 jit_solution(4263431200625416276)
XLA Ops:
  7.2 0.0 copy-start
  7.2 0.0 all-gather.3.cloned.1.call-start
  7.2 1.5 multiply_reduce_fusion.2
  8.7 4.5 convolution_convert_fusion.1
  13.3 4.3 copy.33
  17.5 2.4 multiply_reduce_fusion.1
  20.0 1.1 fusion.6
  21.0 0.0 copy-start.5
  21.0 0.0 copy-start.11
  21.1 2.5 fusion.25
  23.6 0.0 copy-done.5
  23.6 0.0 copy-done.11
  23.6 0.7 fusion.21
  24.3 0.0 copy-done
  24.3 0.0 copy-done.12
  24.3 3.5 convolution_convert_fusion
  27.9 4.8 copy.40
  32.7 0.1 multiply_reduce_fusion.4
  32.8 0.1 rsqrt.54
  32.9 0.0 copy-done.8
  32.9 0.5 fusion.35
  33.5 0.2 reshape.138
  33.7 2.0 fusion.85
  35.6 0.3 fusion.56
  35.9 0.1 copy-done.2
  36.0 0.6 fusion.31
  36.6 0.1 copy.44
  36.8 0.2 reshape.140
  36.9 0.1 fusion.70
  37.1 0.1 fusion.72
  37.2 10.7 %all_gather.9 = bf16[192,1024]{1,0:T(8,128)(2,1)S(1)} all-gather(bf16[48,1024]{1,0:T(8,128)(2,1)S(1)} %fusion.72), channel_id=1, replica_groups=mesh['dp'=64,'lat'=4] {'lat'}, dimensions={0}, use_global_device_ids=true | all-gather | bytes 491520 | tf_op jit(solution)/shard_map/all_gather | solution.py:103
  47.9 2.0 convolution_convert_fusion.5
  49.8 0.0 all-gather.3.cloned.1.call-update
  49.9 0.0 all-gather.5.cloned.1.call-start
  49.9 2.0 convolution_convert_fusion.4
  51.9 0.0 all-gather.5.cloned.1.call-update
  51.9 0.2 reduce-scatter.2.cloned.1.call-start
  52.1 1.3 convolution_convert_fusion.6
  53.4 0.1 copy.45
  53.5 262.9 %all-gather.3.cloned.1.call-done = bf16[12288,256]{1,0:T(8,128)(2,1)} async-done(((bf16[192,256]{1,0:T(8,128)(2,1)}), bf16[12288,256]{1,0:T(8,128)(2,1)}) %all-gather.3.cloned.1.call-update) | async-done | bytes 6291472 | tf_op jit(solution)/shard_map/all_gather | solution.py:122
  316.4 8.7 %copy.46 = bf16[12288,256]{0,1:T(8,128)(2,1)} copy(bf16[12288,256]{1,0:T(8,128)(2,1)} %all-gather.3.cloned.1.call-done) | data formatting | bytes 12582912 | tf_op jit(solution)/shard_map/all_gather | solution.py:122
  325.1 16.6 %multiply_reduce_fusion = (f32[4,192]{1,0:T(4,128)S(1)}, f32[4,192,12288]{2,1,0:T(8,128)}) fusion(bf16[192,4,64]{0,2,1:T(8,128)(2,1)S(1)} %bitcast.138, bf16[12288,4,64]{0,2,1:T(8,128)(2,1)} %bitcast.127), kind=kOutput, calls=%fused_computation.1 | convolution fusion | flops 1226833152 | bytes 44141568 | tf_op jit(solution)/shard_map/qhe,khe->hqk/dot_general | solution.py:62
  341.7 15.9 %fusion = f32[4,192]{1,0:T(4,128)S(1)} fusion(f32[4,192,12288]{2,1,0:T(8,128)} %get-tuple-element.15, f32[4,192]{1,0:T(4,128)S(1)} %broadcast_maximum_fusion), kind=kLoop, calls=%fused_computation.2 | loop fusion | flops 28310784 | bytes 37754880 | tf_op jit(solution)/shard_map/reduce_sum | solution.py:67
  357.6 266.3 %all-gather.5.cloned.1.call-done = bf16[12288,256]{1,0:T(8,128)(2,1)} async-done(((bf16[192,256]{1,0:T(8,128)(2,1)}), bf16[12288,256]{1,0:T(8,128)(2,1)}) %all-gather.5.cloned.1.call-update) | async-done | bytes 6291472 | tf_op jit(solution)/shard_map/all_gather | solution.py:123
  623.9 8.7 %copy.47 = bf16[12288,256]{0,1:T(8,128)(2,1)} copy(bf16[12288,256]{1,0:T(8,128)(2,1)} %all-gather.5.cloned.1.call-done) | data formatting | bytes 12582912 | tf_op jit(solution)/shard_map/all_gather | solution.py:123
  632.6 16.4 %fusion.44 = bf16[192,4,64]{0,2,1:T(8,128)(2,1)S(1)} fusion(bf16[12288,4,64]{0,2,1:T(8,128)(2,1)} %bitcast.126, f32[4,192,12288]{2,1,0:T(8,128)} %get-tuple-element.15, f32[4,192]{1,0:T(4,128)S(1)} %broadcast_maximum_fusion, f32[192,4]{0,1:T(4,128)S(1)} %bitcast.141), kind=kOutput, calls=%fused_computation.54 | convolution fusion | flops 1236369408 | bytes 44144640 | tf_op jit(solution)/shard_map/hqk,khe->hqe/dot_general | solution.py:68
  649.0 0.0 copy-done.6
  649.0 1.0 convolution_convert_fusion.3
  650.0 0.0 reduce-scatter.2.cloned.1.call-update
  650.0 0.0 copy-start.9
  650.1 1.7 convolution_convert_fusion.2
  651.7 0.3 copy.39
  652.0 70.5 %reduce-scatter.2.cloned.1.call-done = bf16[48,1024]{1,0:T(8,128)(2,1)} async-done(((bf16[192,1024]{1,0:T(8,128)(2,1)}), bf16[48,1024]{1,0:T(8,128)(2,1)}) %reduce-scatter.2.cloned.1.call-update) | async-done | bytes 98320 | tf_op jit(solution)/shard_map/reduce_scatter | solution.py:133
  722.5 1.0 multiply_reduce_fusion.3
  723.5 0.0 copy-start.7
  723.5 0.1 rsqrt.57
  723.6 2.1 fusion.38
  725.8 0.2 reshape.145
  726.0 0.2 fusion.86
  726.2 0.1 fusion.68
  726.3 0.0 copy-done.7
  726.3 1.6 bitcast_divide_fusion
  727.9 3.2 copy.50
  731.1 2.5 fusion.22
  (23 shorter events, 0.1 us)
Async XLA Ops:
  7.2 17.2 %copy-start = (bf16[512,2048]{1,0:T(8,128)(2,1)S(1)}, bf16[512,2048]{1,0:T(8,128)(2,1)}, u32[]{:S(2)}) copy-start(bf16[512,2048]{1,0:T(8,128)(2,1)} %param.22) | copy-start | bytes 6291460
  7.2 309.3 %all-gather.3.cloned.1.call-start = ((), (), s32[]{:S(2)}) async-start(), calls=%async_computation.1 | async-start | bytes 6389760 | tf_op jit(solution)/shard_map/all_gather | solution.py:122
  21.0 2.5 copy-start.5
  21.0 2.5 copy-start.11
  23.5 0.8 copy-start.12
  27.9 4.9 copy-start.4
  27.9 5.1 copy-start.3
  27.9 5.1 copy-start.8
  33.6 2.4 copy-start.2
  36.0 1.0 copy-start.10
  49.9 574.1 %all-gather.5.cloned.1.call-start = ((), (), s32[]{:S(2)}) async-start(), calls=%async_computation.2 | async-start | bytes 6389760 | tf_op jit(solution)/shard_map/all_gather | solution.py:123
  51.9 670.6 %reduce-scatter.2.cloned.1.call-start = ((), (), s32[]{:S(2)}) async-start(), calls=%async_computation.3 | async-start | bytes 491520 | tf_op jit(solution)/shard_map/reduce_scatter | solution.py:133
  632.6 16.4 %copy-start.6 = (bf16[256,1024]{1,0:T(8,128)(2,1)S(1)}, bf16[256,1024]{1,0:T(8,128)(2,1)}, u32[]{:S(2)}) copy-start(bf16[256,1024]{1,0:T(8,128)(2,1)} %param.27) | copy-start | bytes 1572868
  632.6 17.5 %copy-start.13 = (f32[512]{0:T(512)S(1)}, f32[512]{0:T(512)}, u32[]{:S(2)}) copy-start(f32[512]{0:T(512)} %param.28) | copy-start | bytes 6148
  650.0 73.6 %copy-start.9 = (f32[1024]{0:T(1024)S(1)}, f32[1024]{0:T(1024)}, u32[]{:S(2)}) copy-start(f32[1024]{0:T(1024)} %param.30) | copy-start | bytes 12292
  723.5 2.8 copy-start.7
  727.9 5.7 copy-start.1
Sparse Core Ops, SparseCore 0:
  50.0 266.4 all-gather.2
  318.8 305.0 all-gather.4
  650.2 72.2 reduce-scatter.1
where the time goes:
time: 741 us; the launch traced here: 740 us
  waiting for transfers between devices  600 us (81%)
  matrix products  61.6 us (8%)
  local copies, waits for them, and re-layouts  31 us (4%)
  other arithmetic  22.8 us (3%)
  between operations  14 us (2%)
  blocking collectives  10.7 us (1%)
    all_gather x1, waiting for transfers between devices, local(): values = lax.all_gather(values_here, 'dp', axis=0, tiled=True)  266 us
    all_gather x1, waiting for transfers between devices, local(): keys = lax.all_gather(keys_here, 'dp', axis=0, tiled=True)  263 us
    reduce_scatter x1, waiting for transfers between devices, local(): lax.psum_scatter(jnp.dot(mixed, w_o_glob, preferred_element_type=jnp.floa...  70.5 us
    dot_general x1, matrix products, fold_update(): jnp.einsum('qhe,khe->hqk', query, keys, preferred_element_type=jnp.float32)  16.6 us
    dot_general x1, matrix products, fold_update(): jnp.einsum('hqk,khe->hqe', weights.astype(jnp.bfloat16), values, preferre...  16.4 us
    reduce_sum x1, other arithmetic, fold_update(): row_total = jnp.sum(weights, axis=-1)  15.9 us
  transfers between devices with their start and end apart: 3, of which 3 were waited for; matrix products, arithmetic and copies ran while one was open for 6% of the time, Pallas kernels for 0%

commit v1 on v0

v1 whole, which is shorter than its diff:
```python
import functools

import jax
import jax.numpy as jnp
import numpy as np
from jax import lax
from jax.experimental import pallas as pl
from jax.experimental.pallas import tpu as pltpu
from jax.sharding import Mesh
from jax.sharding import PartitionSpec as P

HEAD = 64
G = 256
NLAT = 16
LOG2E = 1.4426950408889634
SCALE = LOG2E * HEAD ** (-0.5)

AXES = ("za", "zb", "zc", "yl", "x", "yh", "core")
SIZES = (2, 2, 2, 2, 4, 2, 2)
LAT = ("yh", "core")
HEADS4 = ("zc", "yl")
KEYS4 = ("za", "zb")
OUT64 = ("zc", "yl", "x", "yh", "core")

f32 = jnp.float32
bf16 = jnp.bfloat16


def dot(a, b):
    return jnp.dot(a, b, preferred_element_type=f32)


def dot_t(a, b):
    return lax.dot_general(a, b, (((1,), (1,)), ((), ())), preferred_element_type=f32)


def norm(values, gain):
    factor = lax.rsqrt(jnp.mean(values * values, axis=-1, keepdims=True) + 1e-06)
    return (values * factor * gain).astype(bf16)


def low_lanes(rows):
    return lax.broadcasted_iota(jnp.int32, (rows, 128), 1) < HEAD


def swap(values):
    return pltpu.roll(values, HEAD, 1)


def front_kernel(
    tok_ref, lat_ref, gself_ref, wqkv_ref, wo_ref, gread_ref, wkv_ref, glat_ref, wq_ref, gglob_ref,
    mid_ref, latmid_ref, normed_ref,
):
    x = tok_ref[...].astype(f32)
    packed = dot(norm(x, gself_ref[...]), wqkv_ref[...]).astype(bf16)
    low = low_lanes(G)
    zero = jnp.zeros((G, 128), bf16)
    one = jnp.ones((G, 128), bf16)
    pairs = []
    for p in range(4):
        q2 = packed[:, p * 128 : (p + 1) * 128]
        k2 = packed[:, 512 + p * 128 : 512 + (p + 1) * 128]
        v2 = packed[:, 1024 + p * 128 : 1024 + (p + 1) * 128]
        halves = []
        for half in range(2):
            here = low if half == 0 else jnp.logical_not(low)
            s = dot_t(jnp.where(here, q2, zero), k2) * SCALE
            w = jnp.exp2(s - jnp.max(s, axis=-1, keepdims=True))
            r = dot(w.astype(bf16), jnp.where(here, v2, one))
            halves.append(r / swap(r))
        pairs.append(jnp.where(low, halves[0], halves[1]).astype(bf16))
    mixed = jnp.concatenate(pairs, axis=1)
    mid = (x + dot(mixed, wo_ref[...])).astype(bf16)
    mid_ref[...] = mid
    kv = dot(norm(mid.astype(f32), gread_ref[...]), wkv_ref[...]).astype(bf16)
    lat = lat_ref[...].astype(f32)
    query = dot(norm(lat, glat_ref[...]), wq_ref[...]).astype(bf16)
    part = lax.broadcasted_iota(jnp.int32, (NLAT, 256), 1) // HEAD
    blocks = []
    for quad in range(4):
        q4 = query[:, quad * 256 : (quad + 1) * 256]
        k4 = kv[:, quad * 256 : (quad + 1) * 256]
        v4 = kv[:, 1024 + quad * 256 : 1024 + (quad + 1) * 256]
        stacked = jnp.concatenate(
            [jnp.where(part == a, q4, jnp.zeros_like(q4)) for a in range(4)], axis=0
        )
        s = dot_t(stacked, k4) * SCALE
        w = jnp.exp2(s - jnp.max(s, axis=-1, keepdims=True))
        r = dot(w.astype(bf16), v4) / jnp.sum(w, axis=-1, keepdims=True)
        got = jnp.zeros((NLAT, 256), f32)
        for a in range(4):
            got = jnp.where(part == a, r[a * NLAT : (a + 1) * NLAT], got)
        blocks.append(got)
    latmid = (lat + jnp.concatenate(blocks, axis=1)).astype(bf16)
    latmid_ref[...] = latmid
    normed_ref[...] = norm(latmid.astype(f32), gglob_ref[...])


def project_kernel(block_ref, w_ref, out_ref):
    block = block_ref[...]
    rows = block.shape[0]
    half = rows // 2
    q = dot(block, w_ref[0]).astype(bf16).astype(f32)
    k = dot(block, w_ref[1]).astype(bf16).astype(f32)
    v = dot(block, w_ref[2]).astype(bf16).astype(f32)
    low = low_lanes(rows)
    lowh = low_lanes(half)
    for pair in range(2):
        lanes = slice(pair * 128, (pair + 1) * 128)
        q2, k2, v2 = q[:, lanes], k[:, lanes], v[:, lanes]
        out_ref[2 * pair, :rows] = jnp.where(low, k2, swap(v2)).astype(bf16)
        out_ref[2 * pair + 1, :rows] = jnp.where(low, swap(k2), v2).astype(bf16)
        out_ref[2 * pair, rows:] = jnp.where(lowh, q2[:half], swap(q2[half:])).astype(bf16)
        out_ref[2 * pair + 1, rows:] = jnp.where(lowh, swap(q2[:half]), q2[half:]).astype(bf16)


def attend_kernel(
    place_ref, own_ref, kv1_ref, kv2_ref, kv3_ref, q1_ref, q2_ref, q3_ref, out_ref, keys, values
):
    rows = kv1_ref.shape[1]
    half = rows // 2
    low = low_lanes(rows)
    lowh = low_lanes(half)
    one = jnp.ones((rows, 128), bf16)
    for k, ref in enumerate((own_ref, kv1_ref, kv2_ref, kv3_ref)):
        for t in range(4):
            at = (k * 4 + t) * rows
            kv = ref[t, :rows]
            keys[at : at + rows, :] = kv
            values[at : at + rows, :] = jnp.where(low, one, kv)
    lane = lax.broadcasted_iota(jnp.int32, (rows, 128), 1)
    me = place_ref[0]
    for k, ref in enumerate((own_ref, q1_ref, q2_ref, q3_ref)):
        start = rows if k == 0 else 0

        def tile(t, carry, k=k, ref=ref, start=start):
            got = ref[t, start : start + half].astype(f32)
            zero = jnp.zeros_like(got)
            query = jnp.concatenate(
                [jnp.where(lowh, got, zero), jnp.where(lowh, swap(got), zero)], axis=0
            ).astype(bf16)
            s = dot_t(query, keys[...])
            peak = jnp.max(s, axis=-1, keepdims=True) * SCALE
            w = jnp.exp2(s * SCALE - peak)
            r = dot(w.astype(bf16), values[...])
            total = jnp.where(low, r, 1.0)
            size = peak + jnp.log2(total)
            hi = size.astype(bf16).astype(f32)
            mid = (size - hi).astype(bf16).astype(f32)
            low_part = size - hi - mid
            stats = jnp.where(lane == 0, hi, jnp.where(lane == 1, mid, low_part))
            out_ref[t, me ^ k] = jnp.where(low, stats, r / swap(r)).astype(bf16)
            return carry

        lax.fori_loop(0, 4, tile, 0)


def back_kernel(
    got_ref, latmid_ref, wo_ref, gwlat_ref, wkv_ref, mid_ref, gwrite_ref, wq_ref, tok_ref, lat_ref
):
    rows = latmid_ref.shape[0]
    low = low_lanes(rows)
    heads = [None] * 16
    for t in range(4):
        for lat in range(4):
            parts = [got_ref[t * 16 + x * 4 + lat].astype(f32) for x in range(4)]
            sizes = [
                jnp.sum(jnp.where(lax.broadcasted_iota(jnp.int32, (rows, 128), 1) < 3, p, 0.0), axis=-1, keepdims=True)
                for p in parts
            ]
            peak = functools.reduce(jnp.maximum, sizes)
            weights = [jnp.exp2(s - peak) for s in sizes]
            total = functools.reduce(lax.add, weights)
            mixed = functools.reduce(lax.add, [p * w for p, w in zip(parts, weights)])
            heads[lat * 4 + t] = mixed / total
    pairs = [jnp.where(low, swap(heads[2 * p]), heads[2 * p + 1]).astype(bf16) for p in range(8)]
    mixed = jnp.concatenate(pairs, axis=1)
    latents = (latmid_ref[...].astype(f32) + dot(mixed, wo_ref[...])).astype(bf16)
    lat_ref[...] = latents
    kv = dot(norm(latents.astype(f32), gwlat_ref[...]), wkv_ref[...]).astype(bf16)
    head_of_row = lax.broadcasted_iota(jnp.int32, (8 * NLAT, 512), 0) // NLAT
    head_of_lane = lax.broadcasted_iota(jnp.int32, (8 * NLAT, 512), 1) // HEAD
    here = head_of_row == head_of_lane
    ones = jnp.where(here, 1.0, 0.0).astype(bf16)
    for g in range(rows // NLAT):
        mid = mid_ref[g * G : (g + 1) * G, :].astype(f32)
        query = dot(norm(mid, gwrite_ref[...]), wq_ref[...]).astype(bf16)
        k = kv[g * NLAT : (g + 1) * NLAT, :512]
        v = kv[g * NLAT : (g + 1) * NLAT, 512:]
        zero = jnp.zeros((8 * NLAT, 512), bf16)
        k8 = jnp.where(here, jnp.concatenate([k] * 8, axis=0), zero)
        v8 = jnp.where(here, jnp.concatenate([v] * 8, axis=0), zero)
        s = (dot_t(k8, query) * SCALE).reshape(8, NLAT, G)
        w = jnp.exp2(s - jnp.max(s, axis=1, keepdims=True)).reshape(8 * NLAT, G).astype(bf16)
        turned = w.T
        written = dot(turned, v8) / dot(turned, ones)
        tok_ref[g * G : (g + 1) * G, :] = (mid + written).astype(bf16)


def params(megabytes):
    return pltpu.CompilerParams(vmem_limit_bytes=megabytes * 1024 * 1024)


def whole(array):
    return pl.BlockSpec(array.shape, lambda *_, n=len(array.shape): (0,) * n)


def local(
    tokens,
    latents,
    gain_self,
    w_qkv_tok,
    w_o_tok,
    gain_read,
    w_kv_read,
    gain_lat,
    w_q_read,
    gain_glob,
    w_qkv_glob,
    w_o_glob,
    gain_write,
    w_q_write,
    gain_wlat,
    w_kv_write,
):
    token_rows, width = tokens.shape
    lat_rows, lat_width = latents.shape
    groups = token_rows // G
    row = lambda gain: gain.reshape(1, -1)
    w_o_all = lax.all_gather(w_o_glob, LAT, axis=0, tiled=True)

    fixed = (
        row(gain_self), w_qkv_tok, w_o_tok, row(gain_read), w_kv_read, row(gain_lat), w_q_read,
        row(gain_glob),
    )
    tokens_mid, latents_mid, normed = pl.pallas_call(
        front_kernel,
        grid=(groups,),
        in_specs=[
            pl.BlockSpec((G, width), lambda g: (g, 0)),
            pl.BlockSpec((NLAT, lat_width), lambda g: (g, 0)),
        ]
        + [whole(a) for a in fixed],
        out_specs=[
            pl.BlockSpec((G, width), lambda g: (g, 0)),
            pl.BlockSpec((NLAT, lat_width), lambda g: (g, 0)),
            pl.BlockSpec((NLAT, lat_width), lambda g: (g, 0)),
        ],
        out_shape=[
            jax.ShapeDtypeStruct(tokens.shape, bf16),
            jax.ShapeDtypeStruct(latents.shape, bf16),
            jax.ShapeDtypeStruct(latents.shape, bf16),
        ],
        compiler_params=params(56),
        name="front",
    )(tokens, latents, *fixed)

    block = lax.all_gather(normed, LAT, axis=0, tiled=True)
    block_rows = block.shape[0]
    half = block_rows // 2
    sent = pl.pallas_call(
        project_kernel,
        out_shape=jax.ShapeDtypeStruct((4, block_rows + half, 128), bf16),
        compiler_params=params(56),
        name="project",
    )(block, w_qkv_glob)
    own = lax.all_to_all(sent, HEADS4, 0, 0, tiled=True)
    own_kv = own[:, :block_rows]
    own_q = own[:, block_rows:]
    others_q = [lax.ppermute(own_q, "x", [(i, i ^ k) for i in range(4)]) for k in (1, 2, 3)]
    others_kv = [lax.ppermute(own_kv, KEYS4, [(i, i ^ k) for i in range(4)]) for k in (1, 2, 3)]
    place = lax.axis_index("x").astype(jnp.int32).reshape(1)
    vmem = pl.BlockSpec(memory_space=pltpu.VMEM)
    partial = pl.pallas_call(
        attend_kernel,
        in_specs=[pl.BlockSpec(memory_space=pltpu.SMEM)] + [vmem] * 7,
        out_specs=vmem,
        out_shape=jax.ShapeDtypeStruct((4, 4, block_rows, 128), bf16),
        scratch_shapes=[
            pltpu.VMEM((16 * block_rows, 128), bf16),
            pltpu.VMEM((16 * block_rows, 128), bf16),
        ],
        compiler_params=params(56),
        name="attend",
    )(place, own, *others_kv, *others_q)
    got = lax.all_to_all(
        partial.reshape(64, lat_rows, 128), OUT64, 0, 0, tiled=True
    )
    tokens_out, latents_out = pl.pallas_call(
        back_kernel,
        out_shape=[
            jax.ShapeDtypeStruct(tokens.shape, bf16),
            jax.ShapeDtypeStruct(latents.shape, bf16),
        ],
        compiler_params=params(56),
        name="back",
    )(
        got, latents_mid, w_o_all, row(gain_wlat), w_kv_write, tokens_mid, row(gain_write), w_q_write
    )
    return (tokens_out, latents_out)


def solution(mesh):
    fine = Mesh(np.asarray(mesh.devices).reshape(SIZES), AXES)
    rows = P(AXES, None)
    placed = (
        rows,
        rows,
        P(),
        P(),
        P(),
        P(),
        P(),
        P(),
        P(),
        P(),
        P(None, None, LAT),
        P(LAT, None),
        P(),
        P(),
        P(),
        P(),
    )
    return jax.shard_map(
        local,
        mesh=fine,
        in_specs=placed,
        out_specs=(rows, rows),
        check_vma=False,
    )
```

time: 741 us -> 139 us (0.19)
  waiting for transfers between devices: 600 us -> 10.8 us
  matrix products: 61.6 us -> 0 us
  Pallas kernels: 0 us -> 50 us
  blocking collectives: 10.7 us -> 51.4 us
  local copies, waits for them, and re-layouts: 31 us -> 0.75 us
  other arithmetic: 22.8 us -> 0 us
  starting transfers between devices: 0.3 us -> 11.8 us
    all_gather x2 -> x1, waiting for transfers between devices: 529 us -> 0.01 us  [local(): w_o_all = lax.all_gather(w_o_glob, LAT, axis=0, tiled=True)]
    reduce_scatter x1 -> x0, waiting for transfers between devices: 70.5 us -> none  [local(): lax.psum_scatter(jnp.dot(mixed, w_o_glob, preferred_element_type=jnp.floa...]
    dot_general x18 -> x0, matrix products: 61.6 us -> none  [the longest x1 16.6 us: fold_update(): jnp.einsum('qhe,khe->hqk', query, keys, preferred_element_type=jnp.float32)]
    pallas_call x0 -> x4, Pallas kernels: none -> 50 us  [the longest x1 20.4 us: local(): pl.pallas_call(attend_kernel, in_specs=[pl.BlockSpec(memory_space=pltpu.S...]
    all_to_all x0 -> x2, blocking collectives: none -> 37.3 us  [the longest x1 27.7 us: local(): lax.all_to_all(partial.reshape(64, lat_rows, 128), OUT64, 0, 0, tiled=True)]
    reduce_sum x8 -> x0, other arithmetic: 20.1 us -> none  [the longest x1 15.9 us: fold_update(): row_total = jnp.sum(weights, axis=-1)]
    all_gather x2 -> x0, local copies, waits for them, and re-layouts: 17.3 us -> none  [the longest x1 8.66 us: local(): keys = lax.all_gather(keys_here, 'dp', axis=0, tiled=True)]
    ppermute x0 -> x6, starting transfers between devices: none -> 11.8 us  [the longest x3 8.16 us: local(): lax.ppermute(own_kv, KEYS4, [(i, i ^ k) for i in range(4)])]
  transfers between devices with their start and end apart: 3 -> 7, of which waited for: 3 -> 4; matrix products, arithmetic and copies ran while one was open for 6% -> 0% of each run, Pallas kernels for 0% -> 31%
where the time goes in v1:
time: 139 us
  blocking collectives  51.4 us (37%)
  Pallas kernels  50 us (36%)
  between operations  14.1 us (10%)
  starting transfers between devices  11.8 us (8%)
  waiting for transfers between devices  10.8 us (8%)
    all_to_all x1, blocking collectives, local(): lax.all_to_all(partial.reshape(64, lat_rows, 128), OUT64, 0, 0, tiled=True)  27.7 us
    pallas_call x1, Pallas kernels, local(): pl.pallas_call(attend_kernel, in_specs=[pl.BlockSpec(memory_space=pltpu.S...  20.4 us
    pallas_call x1, Pallas kernels, local(): pl.pallas_call(front_kernel, grid=(groups,), in_specs=[pl.BlockSpec((G, w...  19.5 us
    all_gather x1, blocking collectives, local(): block = lax.all_gather(normed, LAT, axis=0, tiled=True)  14 us
    all_to_all x1, blocking collectives, local(): own = lax.all_to_all(sent, HEADS4, 0, 0, tiled=True)  9.62 us
    ppermute x3, starting transfers between devices, local(): lax.ppermute(own_kv, KEYS4, [(i, i ^ k) for i in range(4)])  8.16 us
    pallas_call x1, Pallas kernels, local(): pl.pallas_call(back_kernel, out_shape=[jax.ShapeDtypeStruct(tokens.shape,...  7.35 us
    ppermute x3, waiting for transfers between devices, local(): lax.ppermute(own_q, 'x', [(i, i ^ k) for i in range(4)])  5.84 us
  transfers between devices with their start and end apart: 7, of which 4 were waited for; matrix products, arithmetic and copies ran while one was open for 0% of the time, Pallas kernels for 31%

profile of v1, /device:TPU:1, one launch (start us, length us, event | category | flops | bytes accessed | tf_op | source)
XLA Modules:
  0.0 138.8 jit_solution(9669670359352829013)
XLA Ops:
  7.2 0.0 all-gather.2.cloned.1.call-start
  7.2 0.7 all-gather.2.cloned.1.call-update
  7.9 19.5 %front.1 = (bf16[768,512]{1,0:T(8,128)(2,1)}, bf16[48,1024]{1,0:T(8,128)(2,1)}, bf16[48,1024]{1,0:T(8,128)(2,1)}) custom-call(bf16[768,512]{1,0:T(8,128)(2,1)} %tok_ref.1, bf16[48,1024]{1,0:T(8,128)(2,1)} %lat_ref.1, f32[1,512]{1,0:T(1,128)} %bitcast.13, bf16[512,1536]{1,0:T(8,128)(2,1)} %wqkv_ref.1, bf16[512,512]{1,0:T(8,128)(2,1)} %wo_ref.1, ...), custom_call_target="tpu_custom_call" | custom-call | tf_op jit(solution)/shard_map/front/pallas_call | solution.py:236
  27.4 14.0 %all_gather.6.block_ref = bf16[192,1024]{1,0:T(8,128)(2,1)} all-gather(bf16[48,1024]{1,0:T(8,128)(2,1)} %get-tuple-element.5), channel_id=1, replica_groups=mesh['za'=2,'zb'=2,'zc'=2,'yl'=2,'x'=4,'yh'=2,'core'=2] {'yh','core'}, dimensions={0}, use_global_device_ids=true | all-gather | bytes 491520 | tf_op jit(solution)/shard_map/all_gather | solution.py:258
  41.4 2.8 %project.1 = bf16[4,288,128]{2,1,0:T(8,128)(2,1)} custom-call(bf16[192,1024]{1,0:T(8,128)(2,1)} %all_gather.6.block_ref, bf16[3,1024,256]{2,1,0:T(8,128)(2,1)} %w_ref.1), custom_call_target="tpu_custom_call" | custom-call | tf_op jit(solution)/shard_map/project/pallas_call | solution.py:261
  44.2 9.6 %all_to_all.10.own_ref = bf16[4,288,128]{2,1,0:T(8,128)(2,1)S(1)} all-to-all(bf16[4,288,128]{2,1,0:T(8,128)(2,1)} %project.1), channel_id=1, replica_groups=mesh['za'=2,'zb'=2,'zc'=2,'yl'=2,'x'=4,'yh'=2,'core'=2] {'zc','yl'}, dimensions={0} | all-to-all | bytes 589824 | tf_op jit(solution)/shard_map/all_to_all | solution.py:267
  53.9 0.0 copy-start
  53.9 1.0 collective-permute-start.3
  54.9 3.0 %collective-permute-start = (bf16[4,192,128]{2,1,0:T(8,128)(2,1)S(1)}, bf16[4,192,128]{2,1,0:T(8,128)(2,1)S(1)}, u32[]{:S(2)}, u32[]{:S(2)}) collective-permute-start(bf16[4,192,128]{2,1,0:T(8,128)(2,1)S(1)} %slice.8), channel_id=1, source_target_pairs={{0,64},{64,0},{128,192},{192,128},{1,65},{65,1},{129,193},{193,129... | collective-permute-start | bytes 589832 | tf_op jit(solution)/shard_map/ppermute | solution.py:271
  57.9 5.1 %collective-permute-start.1 = (bf16[4,192,128]{2,1,0:T(8,128)(2,1)S(1)}, bf16[4,192,128]{2,1,0:T(8,128)(2,1)S(1)}, u32[]{:S(2)}, u32[]{:S(2)}) collective-permute-start(bf16[4,192,128]{2,1,0:T(8,128)(2,1)S(1)} %slice.8), channel_id=1, source_target_pairs={{0,128},{64,192},{128,0},{192,64},{1,129},{65,193},{129,1},{193,65... | collective-permute-start | bytes 589832 | tf_op jit(solution)/shard_map/ppermute | solution.py:271
  63.0 0.0 collective-permute-start.2
  63.0 2.5 %collective-permute-start.4 = (bf16[4,96,128]{2,1,0:T(8,128)(2,1)S(1)}, bf16[4,96,128]{2,1,0:T(8,128)(2,1)S(1)}, u32[]{:S(2)}, u32[]{:S(2)}) collective-permute-start(bf16[4,96,128]{2,1,0:T(8,128)(2,1)S(1)} %slice.9), channel_id=1, source_target_pairs={{0,8},{4,12},{8,0},{12,4},{1,9},{5,13},{9,1},{13,5},{2,10},{6,14},... | collective-permute-start | bytes 294920 | tf_op jit(solution)/shard_map/ppermute | solution.py:270
  65.5 0.0 collective-permute-done.3.q1_ref
  65.5 0.0 copy-start.4
  65.5 0.2 collective-permute-start.5
  65.7 2.3 %collective-permute-done.4.q2_ref = bf16[4,96,128]{2,1,0:T(8,128)(2,1)S(1)} collective-permute-done((bf16[4,96,128]{2,1,0:T(8,128)(2,1)S(1)}, bf16[4,96,128]{2,1,0:T(8,128)(2,1)S(1)}, u32[]{:S(2)}, u32[]{:S(2)}) %collective-permute-start.4) | collective-permute-done | bytes 98336 | tf_op jit(solution)/shard_map/ppermute | solution.py:270
  68.0 0.0 copy-start.5
  68.0 3.5 %collective-permute-done.5.q3_ref = bf16[4,96,128]{2,1,0:T(8,128)(2,1)S(1)} collective-permute-done((bf16[4,96,128]{2,1,0:T(8,128)(2,1)S(1)}, bf16[4,96,128]{2,1,0:T(8,128)(2,1)S(1)}, u32[]{:S(2)}, u32[]{:S(2)}) %collective-permute-start.5) | collective-permute-done | bytes 98336 | tf_op jit(solution)/shard_map/ppermute | solution.py:270
  71.5 0.0 copy-start.6
  71.5 3.9 %collective-permute-done.kv1_ref = bf16[4,192,128]{2,1,0:T(8,128)(2,1)S(1)} collective-permute-done((bf16[4,192,128]{2,1,0:T(8,128)(2,1)S(1)}, bf16[4,192,128]{2,1,0:T(8,128)(2,1)S(1)}, u32[]{:S(2)}, u32[]{:S(2)}) %collective-permute-start) | collective-permute-done | bytes 196640 | tf_op jit(solution)/shard_map/ppermute | solution.py:271
  75.5 0.0 copy-start.1
  75.5 0.4 collective-permute-done.1.kv2_ref
  75.8 0.0 copy-start.2
  75.8 0.0 collective-permute-done.2.kv3_ref
  75.8 0.0 copy-start.3
  75.8 0.0 copy-done
  75.8 0.0 copy-done.4
  75.9 0.0 copy-done.5
  75.9 0.0 copy-done.6
  75.9 0.3 copy-done.1
  76.1 0.4 copy-done.2
  76.5 0.1 copy-done.3
  76.6 20.4 %attend.1 = bf16[4,4,192,128]{3,2,1,0:T(8,128)(2,1)} custom-call(s32[1]{0:T(128)} %bitcast.place_ref, bf16[4,288,128]{2,1,0:T(8,128)(2,1)} %copy-done, bf16[4,192,128]{2,1,0:T(8,128)(2,1)} %copy-done.1, bf16[4,192,128]{2,1,0:T(8,128)(2,1)} %copy-done.2, bf16[4,192,128]{2,1,0:T(8,128)(2,1)} %copy-done.3, bf16[4,96,128]{2,1,0:T(8,128)(2,1)} %copy-done.4, ...), custom_call_target="tpu_custom_call" | custom-call | tf_op jit(solution)/shard_map/attend/pallas_call | solution.py:274
  96.9 27.7 %all_to_all.11.got_ref = bf16[64,48,128]{2,1,0:T(8,128)(2,1)} all-to-all(bf16[64,48,128]{2,1,0:T(8,128)(2,1)} %bitcast.8), channel_id=1, replica_groups=mesh['za'=2,'zb'=2,'zc'=2,'yl'=2,'x'=4,'yh'=2,'core'=2] {'zc','yl','x','..., dimensions={0} | all-to-all | bytes 1572864 | tf_op jit(solution)/shard_map/all_to_all | solution.py:286
  124.6 0.0 all-gather.2.cloned.1.call-done.wo_ref
  124.6 7.4 %back.1 = (bf16[768,512]{1,0:T(8,128)(2,1)}, bf16[48,1024]{1,0:T(8,128)(2,1)}) custom-call(bf16[64,48,128]{2,1,0:T(8,128)(2,1)} %all_to_all.11.got_ref, bf16[48,1024]{1,0:T(8,128)(2,1)} %get-tuple-element.6.latmid_ref, bf16[1024,1024]{1,0:T(8,128)(2,1)} %all-gather.2.cloned.1.call-done.wo_ref, f32[1,1024]{1,0:T(1,128)} %bitcast.11, ...), custom_call_target="tpu_custom_call" | custom-call | tf_op jit(solution)/shard_map/back/pallas_call | solution.py:289
  (2 shorter events, 0.0 us)
Async XLA Ops:
  7.2 117.5 %all-gather.2.cloned.1.call-start = ((), (), s32[]{:S(2)}) async-start(), calls=%async_computation.2 | async-start | bytes 2621440 | tf_op jit(solution)/shard_map/all_gather | solution.py:230
  53.9 22.0 %copy-start = (bf16[4,288,128]{2,1,0:T(8,128)(2,1)}, bf16[4,288,128]{2,1,0:T(8,128)(2,1)S(1)}, u32[]{:S(2)}) copy-start(bf16[4,288,128]{2,1,0:T(8,128)(2,1)S(1)} %all_to_all.10.own_ref) | copy-start | bytes 884740
  53.9 11.6 %collective-permute-start.3 = (bf16[4,96,128]{2,1,0:T(8,128)(2,1)S(1)}, bf16[4,96,128]{2,1,0:T(8,128)(2,1)S(1)}, u32[]{:S(2)}, u32[]{:S(2)}) collective-permute-start(bf16[4,96,128]{2,1,0:T(8,128)(2,1)S(1)} %slice.9), channel_id=1, source_target_pairs={{0,4},{4,0},{8,12},{12,8},{1,5},{5,1},{9,13},{13,9},{2,6},{6,2},{1... | collective-permute-start | bytes 294920 | tf_op jit(solution)/shard_map/ppermute | solution.py:270
  54.9 20.6 %collective-permute-start = (bf16[4,192,128]{2,1,0:T(8,128)(2,1)S(1)}, bf16[4,192,128]{2,1,0:T(8,128)(2,1)S(1)}, u32[]{:S(2)}, u32[]{:S(2)}) collective-permute-start(bf16[4,192,128]{2,1,0:T(8,128)(2,1)S(1)} %slice.8), channel_id=1, source_target_pairs={{0,64},{64,0},{128,192},{192,128},{1,65},{65,1},{129,193},{193,129... | collective-permute-start | bytes 589832 | tf_op jit(solution)/shard_map/ppermute | solution.py:271
  57.9 17.9 %collective-permute-start.1 = (bf16[4,192,128]{2,1,0:T(8,128)(2,1)S(1)}, bf16[4,192,128]{2,1,0:T(8,128)(2,1)S(1)}, u32[]{:S(2)}, u32[]{:S(2)}) collective-permute-start(bf16[4,192,128]{2,1,0:T(8,128)(2,1)S(1)} %slice.8), channel_id=1, source_target_pairs={{0,128},{64,192},{128,0},{192,64},{1,129},{65,193},{129,1},{193,65... | collective-permute-start | bytes 589832 | tf_op jit(solution)/shard_map/ppermute | solution.py:271
  63.0 12.8 %collective-permute-start.2 = (bf16[4,192,128]{2,1,0:T(8,128)(2,1)S(1)}, bf16[4,192,128]{2,1,0:T(8,128)(2,1)S(1)}, u32[]{:S(2)}, u32[]{:S(2)}) collective-permute-start(bf16[4,192,128]{2,1,0:T(8,128)(2,1)S(1)} %slice.8), channel_id=1, source_target_pairs={{0,192},{64,128},{128,64},{192,0},{1,193},{65,129},{129,65},{193,1... | collective-permute-start | bytes 589832 | tf_op jit(solution)/shard_map/ppermute | solution.py:271
  63.0 5.0 %collective-permute-start.4 = (bf16[4,96,128]{2,1,0:T(8,128)(2,1)S(1)}, bf16[4,96,128]{2,1,0:T(8,128)(2,1)S(1)}, u32[]{:S(2)}, u32[]{:S(2)}) collective-permute-start(bf16[4,96,128]{2,1,0:T(8,128)(2,1)S(1)} %slice.9), channel_id=1, source_target_pairs={{0,8},{4,12},{8,0},{12,4},{1,9},{5,13},{9,1},{13,5},{2,10},{6,14},... | collective-permute-start | bytes 294920 | tf_op jit(solution)/shard_map/ppermute | solution.py:270
  65.5 10.3 %copy-start.4 = (bf16[4,96,128]{2,1,0:T(8,128)(2,1)}, bf16[4,96,128]{2,1,0:T(8,128)(2,1)S(1)}, u32[]{:S(2)}) copy-start(bf16[4,96,128]{2,1,0:T(8,128)(2,1)S(1)} %collective-permute-done.3.q1_ref) | copy-start | bytes 294916
  65.5 6.0 %collective-permute-start.5 = (bf16[4,96,128]{2,1,0:T(8,128)(2,1)S(1)}, bf16[4,96,128]{2,1,0:T(8,128)(2,1)S(1)}, u32[]{:S(2)}, u32[]{:S(2)}) collective-permute-start(bf16[4,96,128]{2,1,0:T(8,128)(2,1)S(1)} %slice.9), channel_id=1, source_target_pairs={{0,12},{4,8},{8,4},{12,0},{1,13},{5,9},{9,5},{13,1},{2,14},{6,10},... | collective-permute-start | bytes 294920 | tf_op jit(solution)/shard_map/ppermute | solution.py:270
  68.0 7.8 %copy-start.5 = (bf16[4,96,128]{2,1,0:T(8,128)(2,1)}, bf16[4,96,128]{2,1,0:T(8,128)(2,1)S(1)}, u32[]{:S(2)}) copy-start(bf16[4,96,128]{2,1,0:T(8,128)(2,1)S(1)} %collective-permute-done.4.q2_ref) | copy-start | bytes 294916
  71.5 4.3 %copy-start.6 = (bf16[4,96,128]{2,1,0:T(8,128)(2,1)}, bf16[4,96,128]{2,1,0:T(8,128)(2,1)S(1)}, u32[]{:S(2)}) copy-start(bf16[4,96,128]{2,1,0:T(8,128)(2,1)S(1)} %collective-permute-done.5.q3_ref) | copy-start | bytes 294916
  75.5 0.7 copy-start.1
  75.8 0.7 copy-start.2
  75.8 0.8 copy-start.3
Sparse Core Ops, SparseCore 0:
  9.8 35.6 all-gather.1

commit v2 on v1

v2 whole, which is shorter than its diff:
```python
import functools

import jax
import jax.numpy as jnp
import numpy as np
from jax import lax
from jax.experimental import pallas as pl
from jax.experimental.pallas import tpu as pltpu
from jax.sharding import Mesh
from jax.sharding import PartitionSpec as P

HEAD = 64
G = 256
NLAT = 16
LOG2E = 1.4426950408889634
SCALE = LOG2E * HEAD ** (-0.5)

AXES = ("za", "zb", "zc", "yl", "x", "yh", "core")
SIZES = (2, 2, 2, 2, 4, 2, 2)
LAT = ("yh", "core")
HEADS4 = ("zc", "yl")
KEYS4 = ("za", "zb")
OUT64 = ("zc", "yl", "x", "yh", "core")

f32 = jnp.float32
bf16 = jnp.bfloat16


def dot(a, b):
    return jnp.dot(a, b, preferred_element_type=f32)


def dot_t(a, b):
    return lax.dot_general(a, b, (((1,), (1,)), ((), ())), preferred_element_type=f32)


def norm(values, gain):
    factor = lax.rsqrt(jnp.mean(values * values, axis=-1, keepdims=True) + 1e-06)
    return (values * factor * gain).astype(bf16)


def low_lanes(rows):
    return lax.broadcasted_iota(jnp.int32, (rows, 128), 1) < HEAD


def swap(values):
    return pltpu.roll(values, HEAD, 1)


def front_kernel(
    tok_ref, lat_ref, gself_ref, gread_ref, glat_ref, gglob_ref, wqkv_hbm, wo_hbm, wkv_hbm, wq_hbm,
    mid_ref, latmid_ref, normed_ref,
    wqkv, wo, wkv, wq, packed, kv, mixed, sems,
):
    copies = [
        pltpu.make_async_copy(source, target, sems.at[i])
        for i, (source, target) in enumerate(
            ((wqkv_hbm, wqkv), (wo_hbm, wo), (wq_hbm, wq), (wkv_hbm, wkv))
        )
    ]
    for copy in copies:
        copy.start()
    groups = tok_ref.shape[0] // G
    x = tok_ref[...].astype(f32)
    normed = norm(x, gself_ref[...])
    copies[0].wait()
    packed[...] = dot(normed, wqkv[...]).astype(bf16)
    low = low_lanes(G)
    zero = jnp.zeros((G, 128), bf16)
    for g in range(groups):
        rows = slice(g * G, (g + 1) * G)
        for p in range(4):
            q2 = packed[rows, p * 128 : (p + 1) * 128]
            k2 = packed[rows, 512 + p * 128 : 512 + (p + 1) * 128]
            v2 = packed[rows, 1024 + p * 128 : 1024 + (p + 1) * 128]
            both = jnp.concatenate([jnp.where(low, q2, zero), jnp.where(low, zero, q2)], axis=0)
            s = dot_t(both, k2) * SCALE
            w = jnp.exp2(s - jnp.max(s, axis=-1, keepdims=True))
            r = dot(w.astype(bf16), v2) / jnp.sum(w, axis=-1, keepdims=True)
            mixed[rows, p * 128 : (p + 1) * 128] = jnp.where(low, r[:G], r[G:]).astype(bf16)
    copies[1].wait()
    mid = (x + dot(mixed[...], wo[...])).astype(bf16)
    mid_ref[...] = mid
    normed = norm(mid.astype(f32), gread_ref[...])
    copies[2].wait()
    lat = lat_ref[...].astype(f32)
    query = dot(norm(lat, glat_ref[...]), wq[...]).astype(bf16)
    copies[3].wait()
    kv[...] = dot(normed, wkv[...]).astype(bf16)
    part = lax.broadcasted_iota(jnp.int32, (NLAT, 256), 1) // HEAD
    for g in range(groups):
        rows = slice(g * G, (g + 1) * G)
        mine = slice(g * NLAT, (g + 1) * NLAT)
        blocks = []
        for quad in range(4):
            q4 = query[mine, quad * 256 : (quad + 1) * 256]
            k4 = kv[rows, quad * 256 : (quad + 1) * 256]
            v4 = kv[rows, 1024 + quad * 256 : 1024 + (quad + 1) * 256]
            stacked = jnp.concatenate(
                [jnp.where(part == a, q4, jnp.zeros_like(q4)) for a in range(4)], axis=0
            )
            s = dot_t(stacked, k4) * SCALE
            w = jnp.exp2(s - jnp.max(s, axis=-1, keepdims=True))
            r = dot(w.astype(bf16), v4) / jnp.sum(w, axis=-1, keepdims=True)
            got = jnp.zeros((NLAT, 256), f32)
            for a in range(4):
                got = jnp.where(part == a, r[a * NLAT : (a + 1) * NLAT], got)
            blocks.append(got)
        latmid = (lat[mine] + jnp.concatenate(blocks, axis=1)).astype(bf16)
        latmid_ref[mine, :] = latmid
        normed_ref[mine, :] = norm(latmid.astype(f32), gglob_ref[...])


def project_kernel(block_ref, w_ref, out_ref):
    block = block_ref[...]
    rows = block.shape[0]
    half = rows // 2
    q = dot(block, w_ref[0]).astype(bf16).astype(f32)
    k = dot(block, w_ref[1]).astype(bf16).astype(f32)
    v = dot(block, w_ref[2]).astype(bf16).astype(f32)
    low = low_lanes(rows)
    lowh = low_lanes(half)
    for pair in range(2):
        lanes = slice(pair * 128, (pair + 1) * 128)
        q2, k2, v2 = q[:, lanes], k[:, lanes], v[:, lanes]
        out_ref[2 * pair, :rows] = jnp.where(low, k2, swap(v2)).astype(bf16)
        out_ref[2 * pair + 1, :rows] = jnp.where(low, swap(k2), v2).astype(bf16)
        out_ref[2 * pair, rows:] = jnp.where(lowh, q2[:half], swap(q2[half:])).astype(bf16)
        out_ref[2 * pair + 1, rows:] = jnp.where(lowh, swap(q2[:half]), q2[half:]).astype(bf16)


def unpack_queries(q_refs, starts, rows, queries):
    half = rows // 2
    low = low_lanes(half)
    for k, (ref, start) in enumerate(zip(q_refs, starts)):
        for t in range(4):
            got = ref[t, start : start + half].astype(f32)
            zero = jnp.zeros_like(got)
            at = (k * 4 + t) * rows
            both = jnp.concatenate(
                [jnp.where(low, got, zero), jnp.where(low, swap(got), zero)], axis=0
            )
            queries[at : at + rows, :] = both.astype(bf16)


def attend_part(queries, key_refs, rows, before, finish):
    keys = jnp.concatenate(
        [ref[t, :rows] for ref in key_refs for t in range(ref.shape[0])], axis=0
    )
    values = jnp.where(low_lanes(keys.shape[0]), jnp.ones_like(keys), keys)
    step = 4 * rows
    for k in range(4):
        at = slice(k * step, (k + 1) * step)
        s = dot_t(queries[at, :], keys) * SCALE
        peak = jnp.max(s, axis=-1, keepdims=True)
        if before is None:
            state = dot(jnp.exp2(s - peak).astype(bf16), values)
        else:
            old_peak = before[1, at, :]
            wide = jnp.maximum(peak, old_peak)
            peak = wide[:, :1]
            state = dot(jnp.exp2(s - peak).astype(bf16), values)
            state = state + before[0, at, :] * jnp.exp2(old_peak - wide)
        finish(k, state, peak)


def keep_state(state_ref, step):
    def keep(k, state, peak):
        state_ref[0, k * step : (k + 1) * step, :] = state
        state_ref[1, k * step : (k + 1) * step, :] = jnp.broadcast_to(peak, state.shape)

    return keep


def attend_first_kernel(own_ref, q1_ref, q2_ref, q3_ref, queries_ref, state_ref):
    rows = q1_ref.shape[1] * 2
    unpack_queries((own_ref, q1_ref, q2_ref, q3_ref), (rows, 0, 0, 0), rows, queries_ref)
    attend_part(queries_ref, (own_ref,), rows, None, keep_state(state_ref, 4 * rows))


def attend_next_kernel(queries_ref, kv1_ref, kv2_ref, before_ref, state_ref):
    rows = kv1_ref.shape[1]
    attend_part(
        queries_ref, (kv1_ref, kv2_ref), rows, before_ref, keep_state(state_ref, 4 * rows)
    )


def attend_last_kernel(place_ref, queries_ref, kv1_ref, kv2_ref, before_ref, out_ref):
    rows = kv1_ref.shape[1]
    unit = rows // 4
    half = unit // 2
    me = place_ref[0]
    low = low_lanes(half)
    lane = lax.broadcasted_iota(jnp.int32, (8, 128), 1)
    term = lax.rem(lane, 3)

    def send(k, state, peak):
        turned = swap(state)
        for t in range(4):
            for u in range(4):
                at = (t * 4 + u) * unit
                top = slice(at, at + half)
                end = slice(at + half, at + unit)
                packed = jnp.where(low, turned[top], state[end]) / jnp.where(
                    low, state[top], turned[end]
                )
                sums = jnp.ones((8, 128), f32)
                peaks = jnp.zeros((8, 128), f32)
                for a in range(unit // 8):
                    here = jnp.logical_and(lane >= 3 * a, lane < 3 * a + 3)
                    part = slice(at + 8 * a, at + 8 * a + 8)
                    sums = jnp.where(here, state[part], sums)
                    peaks = jnp.where(here, peak[part], peaks)
                size = peaks + jnp.log2(sums)
                first = size.astype(bf16).astype(f32)
                second = (size - first).astype(bf16).astype(f32)
                stats = jnp.where(
                    term == 0, first, jnp.where(term == 1, second, size - first - second)
                )
                out_ref[t, me ^ k, u * 32 : (u + 1) * 32] = jnp.concatenate(
                    [packed, stats], axis=0
                ).astype(bf16)

    attend_part(queries_ref, (kv1_ref, kv2_ref), rows, before_ref, send)


def write_query_kernel(mid_ref, gain_ref, w_ref, out_ref):
    out_ref[...] = dot(norm(mid_ref[...].astype(f32), gain_ref[...]), w_ref[...]).astype(bf16)


def back_kernel(
    got_ref, latmid_ref, gwlat_ref, mid_ref, query_ref, wo_hbm, wkv_hbm, tok_ref, lat_ref,
    wo, wkv, sems,
):
    copies = [
        pltpu.make_async_copy(source, target, sems.at[i])
        for i, (source, target) in enumerate(((wo_hbm, wo), (wkv_hbm, wkv)))
    ]
    for copy in copies:
        copy.start()
    rows = latmid_ref.shape[0]
    half = rows // 2
    low = low_lanes(half)
    low8 = low_lanes(8)
    heads = [None] * 16
    for t in range(4):
        for lat in range(4):
            parts = [got_ref[t * 16 + x * 4 + lat].astype(f32) for x in range(4)]
            sizes = [
                p[half:] + pltpu.roll(p[half:], 127, 1) + pltpu.roll(p[half:], 126, 1)
                for p in parts
            ]
            peak = functools.reduce(jnp.maximum, sizes)
            weights = [jnp.exp2(s - peak) for s in sizes]
            total = functools.reduce(lax.add, weights)
            mixed = jnp.zeros((half, 128), f32)
            for p, w in zip(parts, weights):
                share = w / total
                spread = [
                    jnp.where(low8, share[:, 3 * b : 3 * b + 1], share[:, c : c + 1])
                    for b, c in ((b, 3 * (b + half // 8)) for b in range(half // 8))
                ]
                mixed = mixed + p[:half] * jnp.concatenate(spread, axis=0)
            heads[lat * 4 + t] = mixed
    pairs = []
    for p in range(8):
        one, two = heads[2 * p], heads[2 * p + 1]
        top = jnp.where(low, one, swap(two))
        end = jnp.where(low, swap(one), two)
        pairs.append(jnp.concatenate([top, end], axis=0).astype(bf16))
    mixed = jnp.concatenate(pairs, axis=1)
    copies[0].wait()
    latents = (latmid_ref[...].astype(f32) + dot(mixed, wo[...])).astype(bf16)
    lat_ref[...] = latents
    normed = norm(latents.astype(f32), gwlat_ref[...])
    copies[1].wait()
    kv = dot(normed, wkv[...]).astype(bf16)
    head_of_row = lax.broadcasted_iota(jnp.int32, (8 * NLAT, 512), 0) // NLAT
    head_of_lane = lax.broadcasted_iota(jnp.int32, (8 * NLAT, 512), 1) // HEAD
    here = head_of_row == head_of_lane
    ones = jnp.where(here, 1.0, 0.0).astype(bf16)
    for g in range(rows // NLAT):
        mid = mid_ref[g * G : (g + 1) * G, :].astype(f32)
        query = query_ref[g * G : (g + 1) * G, :]
        k = kv[g * NLAT : (g + 1) * NLAT, :512]
        v = kv[g * NLAT : (g + 1) * NLAT, 512:]
        zero = jnp.zeros((8 * NLAT, 512), bf16)
        k8 = jnp.where(here, jnp.concatenate([k] * 8, axis=0), zero)
        v8 = jnp.where(here, jnp.concatenate([v] * 8, axis=0), zero)
        s = (dot_t(k8, query) * SCALE).reshape(8, NLAT, G)
        w = jnp.exp2(s - jnp.max(s, axis=1, keepdims=True)).reshape(8 * NLAT, G).astype(bf16)
        turned = w.T
        written = dot(turned, v8) / dot(turned, ones)
        tok_ref[g * G : (g + 1) * G, :] = (mid + written).astype(bf16)


def params(megabytes):
    return pltpu.CompilerParams(vmem_limit_bytes=megabytes * 1024 * 1024)


def cost(flops, bytes_accessed, transcendentals=0):
    return pl.CostEstimate(
        flops=int(flops), bytes_accessed=int(bytes_accessed), transcendentals=int(transcendentals)
    )


def local(
    tokens,
    latents,
    gain_self,
    w_qkv_tok,
    w_o_tok,
    gain_read,
    w_kv_read,
    gain_lat,
    w_q_read,
    gain_glob,
    w_qkv_glob,
    w_o_glob,
    gain_write,
    w_q_write,
    gain_wlat,
    w_kv_write,
):
    token_rows, width = tokens.shape
    lat_rows, lat_width = latents.shape
    row = lambda gain: gain.reshape(1, -1)
    vmem = pl.BlockSpec(memory_space=pltpu.VMEM)
    hbm = pl.BlockSpec(memory_space=pl.ANY)
    weights = (w_qkv_tok, w_o_tok, w_kv_read, w_q_read)
    tokens_mid, latents_mid, normed = pl.pallas_call(
        front_kernel,
        in_specs=[vmem] * 6 + [hbm] * 4,
        out_specs=[vmem] * 3,
        out_shape=[
            jax.ShapeDtypeStruct(tokens.shape, bf16),
            jax.ShapeDtypeStruct(latents.shape, bf16),
            jax.ShapeDtypeStruct(latents.shape, bf16),
        ],
        scratch_shapes=[pltpu.VMEM(w.shape, bf16) for w in weights]
        + [
            pltpu.VMEM((token_rows, w_qkv_tok.shape[1]), bf16),
            pltpu.VMEM((token_rows, w_kv_read.shape[1]), bf16),
            pltpu.VMEM((token_rows, width), bf16),
            pltpu.SemaphoreType.DMA((4,)),
        ],
        compiler_params=params(60),
        name="front",
    )(
        tokens, latents, row(gain_self), row(gain_read), row(gain_lat), row(gain_glob), *weights
    )

    block = lax.all_gather(normed, LAT, axis=0, tiled=True)
    block_rows = block.shape[0]
    half = block_rows // 2
    sent = pl.pallas_call(
        project_kernel,
        in_specs=[vmem] * 2,
        out_specs=vmem,
        out_shape=jax.ShapeDtypeStruct((4, block_rows + half, 128), bf16),
        compiler_params=params(32),
        name="project",
    )(block, w_qkv_glob)
    own = lax.all_to_all(sent, HEADS4, 0, 0, tiled=True)
    own, w_o_here = lax.optimization_barrier((own, w_o_glob))
    w_o_all = lax.all_gather(w_o_here, LAT, axis=0, tiled=True)
    own_kv = own[:, :block_rows]
    own_q = own[:, block_rows:]
    others_q = [lax.ppermute(own_q, "x", [(i, i ^ k) for i in range(4)]) for k in (1, 2, 3)]
    ahead = [(i, (i + 1) % 4) for i in range(4)]
    behind = [(i, (i - 1) % 4) for i in range(4)]
    kv_ahead = lax.ppermute(own_kv, KEYS4, ahead)
    kv_behind = lax.ppermute(own_kv, KEYS4, behind)
    kv_far1 = lax.ppermute(kv_ahead[:2], KEYS4, ahead)
    kv_far2 = lax.ppermute(kv_behind[2:], KEYS4, behind)
    place = lax.axis_index("x").astype(jnp.int32).reshape(1)
    many = 16 * block_rows

    def part_cost(parts):
        return cost(parts * many * many * 64, many * 128 * 10, parts * many * many // 4)

    queries, state = pl.pallas_call(
        attend_first_kernel,
        in_specs=[vmem] * 4,
        out_specs=[vmem] * 2,
        out_shape=[
            jax.ShapeDtypeStruct((many, 128), bf16),
            jax.ShapeDtypeStruct((2, many, 128), f32),
        ],
        compiler_params=params(32),
        cost_estimate=part_cost(1),
        name="attend_first",
    )(own, *others_q)
    state = pl.pallas_call(
        attend_next_kernel,
        in_specs=[vmem] * 4,
        out_specs=vmem,
        out_shape=jax.ShapeDtypeStruct((2, many, 128), f32),
        compiler_params=params(32),
        cost_estimate=part_cost(2),
        name="attend_next",
    )(queries, kv_ahead, kv_behind, state)
    message = 2 * lat_rows // 3
    partial = pl.pallas_call(
        attend_last_kernel,
        in_specs=[pl.BlockSpec(memory_space=pltpu.SMEM)] + [vmem] * 4,
        out_specs=vmem,
        out_shape=jax.ShapeDtypeStruct((4, 4, 4 * message, 128), bf16),
        compiler_params=params(32),
        cost_estimate=part_cost(1),
        name="attend_last",
    )(place, queries, kv_far1, kv_far2, state)
    got = lax.all_to_all(partial.reshape(64, message, 128), OUT64, 0, 0, tiled=True)
    tokens_late, partial = lax.optimization_barrier((tokens_mid, partial))
    query = pl.pallas_call(
        write_query_kernel,
        in_specs=[vmem] * 3,
        out_specs=vmem,
        out_shape=jax.ShapeDtypeStruct(tokens.shape, bf16),
        compiler_params=params(32),
        cost_estimate=cost(2 * token_rows * width * width, token_rows * width * 4),
        name="write_query",
    )(tokens_late, row(gain_write), w_q_write)
    tokens_out, latents_out = pl.pallas_call(
        back_kernel,
        in_specs=[vmem] * 5 + [hbm] * 2,
        out_specs=[vmem] * 2,
        out_shape=[
            jax.ShapeDtypeStruct(tokens.shape, bf16),
            jax.ShapeDtypeStruct(latents.shape, bf16),
        ],
        scratch_shapes=[
            pltpu.VMEM(w_o_all.shape, bf16),
            pltpu.VMEM(w_kv_write.shape, bf16),
            pltpu.SemaphoreType.DMA((2,)),
        ],
        compiler_params=params(51),
        name="back",
    )(got, latents_mid, row(gain_wlat), tokens_late, query, w_o_all, w_kv_write)
    return (tokens_out, latents_out)


def solution(mesh):
    fine = Mesh(np.asarray(mesh.devices).reshape(SIZES), AXES)
    rows = P(AXES, None)
    placed = (
        rows,
        rows,
        P(),
        P(),
        P(),
        P(),
        P(),
        P(),
        P(),
        P(),
        P(None, None, LAT),
        P(LAT, None),
        P(),
        P(),
        P(),
        P(),
    )
    return jax.shard_map(
        local,
        mesh=fine,
        in_specs=placed,
        out_specs=(rows, rows),
        check_vma=False,
    )
```

time: 139 us -> 111 us (0.80)
  blocking collectives: 51.4 us -> 19.5 us
  Pallas kernels: 50 us -> 38.4 us
  starting transfers between devices: 11.8 us -> 20.8 us
  waiting for transfers between devices: 10.8 us -> 17.7 us
    all_to_all x1 -> x0, blocking collectives: 27.7 us -> none  [local(): lax.all_to_all(partial.reshape(64, lat_rows, 128), OUT64, 0, 0, tiled=True)]
    all_to_all x0 -> x1, waiting for transfers between devices: none -> 12 us  [local(): lax.all_to_all(partial.reshape(64, message, 128), OUT64, 0, 0, tiled=True)]
    pallas_call x4 -> x7, Pallas kernels: 50 us -> 38.4 us  [the longest x1 13.2 us: local(): pl.pallas_call(front_kernel, in_specs=[vmem] * 6 + [hbm] * 4, out_specs=[...]
    all_to_all x0 -> x1, starting transfers between devices: none -> 8.73 us  [local(): lax.all_to_all(partial.reshape(64, message, 128), OUT64, 0, 0, tiled=True)]
    ppermute x3 -> x4, waiting for transfers between devices: 4.3 us -> 0.01 us  [the longest x1 0.01 us: local(): kv_ahead = lax.ppermute(own_kv, KEYS4, ahead)]
    all_gather x1, blocking collectives: 14 us -> 10.9 us  [local(): block = lax.all_gather(normed, LAT, axis=0, tiled=True)]
    ppermute x3 -> x4, starting transfers between devices: 8.16 us -> 8.12 us  [the longest x1 2.4 us: local(): kv_far2 = lax.ppermute(kv_behind[2:], KEYS4, behind)]
  transfers between devices with their start and end apart: 7 -> 9, of which waited for: 4 -> 3; matrix products, arithmetic and copies ran while one was open for 0% -> 0% of each run, Pallas kernels for 31% -> 16%
where the time goes in v2:
time: 111 us
  Pallas kernels  38.4 us (35%)
  starting transfers between devices  20.8 us (19%)
  blocking collectives  19.5 us (18%)
  waiting for transfers between devices  17.7 us (16%)
  between operations  14.2 us (13%)
    pallas_call x1, Pallas kernels, local(): pl.pallas_call(front_kernel, in_specs=[vmem] * 6 + [hbm] * 4, out_specs=[...  13.2 us
    all_to_all x1, waiting for transfers between devices, local(): lax.all_to_all(partial.reshape(64, message, 128), OUT64, 0, 0, tiled=True)  12 us
    all_gather x1, blocking collectives, local(): block = lax.all_gather(normed, LAT, axis=0, tiled=True)  10.9 us
    all_to_all x1, starting transfers between devices, local(): lax.all_to_all(partial.reshape(64, message, 128), OUT64, 0, 0, tiled=True)  8.73 us
    all_to_all x1, blocking collectives, local(): own = lax.all_to_all(sent, HEADS4, 0, 0, tiled=True)  8.59 us
    pallas_call x1, Pallas kernels, local(): pl.pallas_call(attend_next_kernel, in_specs=[vmem] * 4, out_specs=vmem, o...  7.67 us
    pallas_call x1, Pallas kernels, local(): pl.pallas_call(back_kernel, in_specs=[vmem] * 5 + [hbm] * 2, out_specs=[v...  7.03 us
    ppermute x3, waiting for transfers between devices, local(): lax.ppermute(own_q, 'x', [(i, i ^ k) for i in range(4)])  5.67 us
  transfers between devices with their start and end apart: 9, of which 3 were waited for; matrix products, arithmetic and copies ran while one was open for 0% of the time, Pallas kernels for 16%

profile of v2, /device:TPU:1, one launch (start us, length us, event | category | flops | bytes accessed | tf_op | source)
XLA Modules:
  0.0 110.7 jit_solution(14276997332034634284)
XLA Ops:
  7.2 0.0 all-gather.2.cloned.1.call-start
  7.2 0.0 copy-start.1
  7.2 13.2 %front.1 = (bf16[768,512]{1,0:T(8,128)(2,1)}, bf16[48,1024]{1,0:T(8,128)(2,1)}, bf16[48,1024]{1,0:T(8,128)(2,1)}) custom-call(bf16[768,512]{1,0:T(8,128)(2,1)} %tok_ref.1, bf16[48,1024]{1,0:T(8,128)(2,1)} %lat_ref.1, f32[1,512]{1,0:T(1,128)} %bitcast.12, f32[1,512]{1,0:T(1,128)} %bitcast.13, f32[1,1024]{1,0:T(1,128)} %bitcast.10, f32[1,1024]{1,0:T(1,128)} %bitcast.11, ...), custom_call_target="tpu_custom_call" | custom-call | tf_op jit(solution)/shard_map/front/pallas_call | solution.py:331
  20.4 10.9 %all_gather.6.block_ref = bf16[192,1024]{1,0:T(8,128)(2,1)S(1)} all-gather(bf16[48,1024]{1,0:T(8,128)(2,1)} %get-tuple-element.10), channel_id=1, replica_groups=mesh['za'=2,'zb'=2,'zc'=2,'yl'=2,'x'=4,'yh'=2,'core'=2] {'yh','core'}, dimensions={0}, use_global_device_ids=true | all-gather | bytes 491520 | tf_op jit(solution)/shard_map/all_gather | solution.py:353
  31.4 0.0 copy-done.1
  31.4 0.6 project.1
  31.9 8.6 %all_to_all.10.own_ref = bf16[4,288,128]{2,1,0:T(8,128)(2,1)S(1)} all-to-all(bf16[4,288,128]{2,1,0:T(8,128)(2,1)S(1)} %project.1), channel_id=1, replica_groups=mesh['za'=2,'zb'=2,'zc'=2,'yl'=2,'x'=4,'yh'=2,'core'=2] {'zc','yl'}, dimensions={0} | all-to-all | bytes 589824 | tf_op jit(solution)/shard_map/all_to_all | solution.py:364
  40.5 0.0 all-gather.2.cloned.1.call-update
  40.6 2.1 %collective-permute-start.3 = (bf16[4,192,128]{2,1,0:T(8,128)(2,1)S(1)}, bf16[4,192,128]{2,1,0:T(8,128)(2,1)S(1)}, u32[]{:S(2)}, u32[]{:S(2)}) collective-permute-start(bf16[4,192,128]{2,1,0:T(8,128)(2,1)S(1)} %slice.13), channel_id=1, source_target_pairs={{0,64},{64,128},{128,192},{192,0},{1,65},{65,129},{129,193},{193,1... | collective-permute-start | bytes 589832 | tf_op jit(solution)/shard_map/ppermute | solution.py:372
  42.6 2.3 %collective-permute-start.5 = (bf16[4,192,128]{2,1,0:T(8,128)(2,1)S(1)}, bf16[4,192,128]{2,1,0:T(8,128)(2,1)S(1)}, u32[]{:S(2)}, u32[]{:S(2)}) collective-permute-start(bf16[4,192,128]{2,1,0:T(8,128)(2,1)S(1)} %slice.13), channel_id=1, source_target_pairs={{0,192},{64,0},{128,64},{192,128},{1,193},{65,1},{129,65},{193,129... | collective-permute-start | bytes 589832 | tf_op jit(solution)/shard_map/ppermute | solution.py:373
  45.0 1.3 %collective-permute-start = (bf16[4,96,128]{2,1,0:T(8,128)(2,1)S(1)}, bf16[4,96,128]{2,1,0:T(8,128)(2,1)S(1)}, u32[]{:S(2)}, u32[]{:S(2)}) collective-permute-start(bf16[4,96,128]{2,1,0:T(8,128)(2,1)S(1)} %slice.12), channel_id=1, source_target_pairs={{0,4},{4,0},{8,12},{12,8},{1,5},{5,1},{9,13},{13,9},{2,6},{6,2},{1... | collective-permute-start | bytes 294920 | tf_op jit(solution)/shard_map/ppermute | solution.py:369
  46.3 2.5 %collective-permute-start.1 = (bf16[4,96,128]{2,1,0:T(8,128)(2,1)S(1)}, bf16[4,96,128]{2,1,0:T(8,128)(2,1)S(1)}, u32[]{:S(2)}, u32[]{:S(2)}) collective-permute-start(bf16[4,96,128]{2,1,0:T(8,128)(2,1)S(1)} %slice.12), channel_id=1, source_target_pairs={{0,8},{4,12},{8,0},{12,4},{1,9},{5,13},{9,1},{13,5},{2,10},{6,14},... | collective-permute-start | bytes 294920 | tf_op jit(solution)/shard_map/ppermute | solution.py:369
  48.7 0.2 collective-permute-start.2
  48.9 0.0 collective-permute-done.q1_ref
  48.9 2.9 %collective-permute-done.1.q2_ref = bf16[4,96,128]{2,1,0:T(8,128)(2,1)S(1)} collective-permute-done((bf16[4,96,128]{2,1,0:T(8,128)(2,1)S(1)}, bf16[4,96,128]{2,1,0:T(8,128)(2,1)S(1)}, u32[]{:S(2)}, u32[]{:S(2)}) %collective-permute-start.1) | collective-permute-done | bytes 98336 | tf_op jit(solution)/shard_map/ppermute | solution.py:369
  51.8 2.8 %collective-permute-done.2.q3_ref = bf16[4,96,128]{2,1,0:T(8,128)(2,1)S(1)} collective-permute-done((bf16[4,96,128]{2,1,0:T(8,128)(2,1)S(1)}, bf16[4,96,128]{2,1,0:T(8,128)(2,1)S(1)}, u32[]{:S(2)}, u32[]{:S(2)}) %collective-permute-start.2) | collective-permute-done | bytes 98336 | tf_op jit(solution)/shard_map/ppermute | solution.py:369
  54.6 3.7 %attend_first.1 = (bf16[3072,128]{1,0:T(8,128)(2,1)S(1)}, f32[2,3072,128]{2,1,0:T(8,128)S(1)}) custom-call(bf16[4,288,128]{2,1,0:T(8,128)(2,1)S(1)} %all_to_all.10.own_ref, bf16[4,96,128]{2,1,0:T(8,128)(2,1)S(1)} %collective-permute-done.q1_ref, bf16[4,96,128]{2,1,0:T(8,128)(2,1)S(1)} %collective-permute-done.1.q2_ref, ...), custom_call_target="tpu_custom_call" | custom-call | flops 603979776 | bytes 3932160 | tf_op jit(solution)/shard_map/attend_first/pallas_call | solution.py:382
  58.3 0.0 collective-permute-done.3.kv1_ref
  58.3 1.3 %collective-permute-start.4 = (bf16[2,192,128]{2,1,0:T(8,128)(2,1)S(1)}, bf16[2,192,128]{2,1,0:T(8,128)(2,1)S(1)}, u32[]{:S(2)}, u32[]{:S(2)}) collective-permute-start(bf16[2,192,128]{2,1,0:T(8,128)(2,1)S(1)} %slice.16), channel_id=1, source_target_pairs={{0,64},{64,128},{128,192},{192,0},{1,65},{65,129},{129,193},{193,1... | collective-permute-start | bytes 294920 | tf_op jit(solution)/shard_map/ppermute | solution.py:374
  59.6 0.0 collective-permute-done.5.kv2_ref
  59.6 2.4 %collective-permute-start.6 = (bf16[2,192,128]{2,1,0:T(8,128)(2,1)S(1)}, bf16[2,192,128]{2,1,0:T(8,128)(2,1)S(1)}, u32[]{:S(2)}, u32[]{:S(2)}) collective-permute-start(bf16[2,192,128]{2,1,0:T(8,128)(2,1)S(1)} %slice.17), channel_id=1, source_target_pairs={{0,192},{64,0},{128,64},{192,128},{1,193},{65,1},{129,65},{193,129... | collective-permute-start | bytes 294920 | tf_op jit(solution)/shard_map/ppermute | solution.py:375
  62.0 7.7 %attend_next.1.before_ref = f32[2,3072,128]{2,1,0:T(8,128)S(1)} custom-call(bf16[3072,128]{1,0:T(8,128)(2,1)S(1)} %get-tuple-element.12.queries_ref, bf16[4,192,128]{2,1,0:T(8,128)(2,1)S(1)} %collective-permute-done.3.kv1_ref, bf16[4,192,128]{2,1,0:T(8,128)(2,1)S(1)} %collective-permute-done.5.kv2_ref, f32[2,3072,128]{2,1,0:T(8,128)S(1)} %get-tuple-element.13.before_ref), custom_call_target="tpu_custom_call" | custom-call | flops 1207959552 | bytes 3932160 | tf_op jit(solution)/shard_map/attend_next/pallas_call | solution.py:394
  69.7 0.0 collective-permute-done.4.kv1_ref
  69.7 0.0 collective-permute-done.6.kv2_ref
  69.7 0.0 copy-start
  69.7 0.0 copy-start.2
  69.7 0.0 copy-start.5
  69.8 5.6 %attend_last.1 = bf16[4,4,128,128]{3,2,1,0:T(8,128)(2,1)} custom-call(s32[1]{0:T(128)} %bitcast.place_ref, bf16[3072,128]{1,0:T(8,128)(2,1)S(1)} %get-tuple-element.12.queries_ref, bf16[2,192,128]{2,1,0:T(8,128)(2,1)S(1)} %collective-permute-done.4.kv1_ref, bf16[2,192,128]{2,1,0:T(8,128)(2,1)S(1)} %collective-permute-done.6.kv2_ref, ...), custom_call_target="tpu_custom_call" | custom-call | flops 603979776 | bytes 3932160 | tf_op jit(solution)/shard_map/attend_last/pallas_call | solution.py:404
  75.4 0.0 copy-start.3
  75.4 0.0 copy-start.4
  75.4 8.7 %all-to-all-start.1 = ((bf16[64,32,128]{2,1,0:T(8,128)(2,1)}), bf16[64,32,128]{2,1,0:T(8,128)(2,1)S(1)}, u32[]{:S(2)}, u32[]{:S(2)}) async-start(bf16[64,32,128]{2,1,0:T(8,128)(2,1)} %bitcast.5), calls=%async_computation.1 | async-start | bytes 1048576 | tf_op jit(solution)/shard_map/all_to_all | solution.py:413
  84.1 0.0 copy-done
  84.1 0.0 copy-done.2
  84.1 0.0 copy-done.5
  84.1 0.6 write_query.1.query_ref
  84.8 12.0 %all-to-all-done.1.got_ref = bf16[64,32,128]{2,1,0:T(8,128)(2,1)S(1)} async-done(((bf16[64,32,128]{2,1,0:T(8,128)(2,1)}), bf16[64,32,128]{2,1,0:T(8,128)(2,1)S(1)}, u32[]{:S(2)}, u32[]{:S(2)}) %all-to-all-start.1) | async-done | bytes 524320 | tf_op jit(solution)/shard_map/all_to_all | solution.py:413
  96.8 0.0 all-gather.2.cloned.1.call-done.wo_hbm
  96.8 0.0 copy-done.3
  96.8 0.0 copy-done.4
  96.8 7.0 %back.1 = (bf16[768,512]{1,0:T(8,128)(2,1)}, bf16[48,1024]{1,0:T(8,128)(2,1)}) custom-call(bf16[64,32,128]{2,1,0:T(8,128)(2,1)S(1)} %all-to-all-done.1.got_ref, bf16[48,1024]{1,0:T(8,128)(2,1)S(1)} %copy-done.3, f32[1,1024]{1,0:T(1,128)S(1)} %bitcast.8, bf16[768,512]{1,0:T(8,128)(2,1)S(1)} %copy-done, bf16[768,512]{1,0:T(8,128)(2,1)S(1)} %write_query.1.query_ref, ...), custom_call_target="tpu_custom_call" | custom-call | tf_op jit(solution)/shard_map/back/pallas_call | solution.py:424
  (4 shorter events, 0.0 us)
Async XLA Ops:
  7.2 89.7 %all-gather.2.cloned.1.call-start = ((), (), s32[]{:S(2)}) async-start(), calls=%async_computation.2 | async-start | bytes 2621440 | tf_op jit(solution)/shard_map/all_gather | solution.py:366
  7.2 24.1 %copy-start.1 = (bf16[3,1024,256]{2,1,0:T(8,128)(2,1)S(1)}, bf16[3,1024,256]{2,1,0:T(8,128)(2,1)}, u32[]{:S(2)}) copy-start(bf16[3,1024,256]{2,1,0:T(8,128)(2,1)} %w_ref.2) | copy-start | bytes 4718596
  40.6 17.7 %collective-permute-start.3 = (bf16[4,192,128]{2,1,0:T(8,128)(2,1)S(1)}, bf16[4,192,128]{2,1,0:T(8,128)(2,1)S(1)}, u32[]{:S(2)}, u32[]{:S(2)}) collective-permute-start(bf16[4,192,128]{2,1,0:T(8,128)(2,1)S(1)} %slice.13), channel_id=1, source_target_pairs={{0,64},{64,128},{128,192},{192,0},{1,65},{65,129},{129,193},{193,1... | collective-permute-start | bytes 589832 | tf_op jit(solution)/shard_map/ppermute | solution.py:372
  42.6 17.0 %collective-permute-start.5 = (bf16[4,192,128]{2,1,0:T(8,128)(2,1)S(1)}, bf16[4,192,128]{2,1,0:T(8,128)(2,1)S(1)}, u32[]{:S(2)}, u32[]{:S(2)}) collective-permute-start(bf16[4,192,128]{2,1,0:T(8,128)(2,1)S(1)} %slice.13), channel_id=1, source_target_pairs={{0,192},{64,0},{128,64},{192,128},{1,193},{65,1},{129,65},{193,129... | collective-permute-start | bytes 589832 | tf_op jit(solution)/shard_map/ppermute | solution.py:373
  45.0 3.9 %collective-permute-start = (bf16[4,96,128]{2,1,0:T(8,128)(2,1)S(1)}, bf16[4,96,128]{2,1,0:T(8,128)(2,1)S(1)}, u32[]{:S(2)}, u32[]{:S(2)}) collective-permute-start(bf16[4,96,128]{2,1,0:T(8,128)(2,1)S(1)} %slice.12), channel_id=1, source_target_pairs={{0,4},{4,0},{8,12},{12,8},{1,5},{5,1},{9,13},{13,9},{2,6},{6,2},{1... | collective-permute-start | bytes 294920 | tf_op jit(solution)/shard_map/ppermute | solution.py:369
  46.3 5.5 %collective-permute-start.1 = (bf16[4,96,128]{2,1,0:T(8,128)(2,1)S(1)}, bf16[4,96,128]{2,1,0:T(8,128)(2,1)S(1)}, u32[]{:S(2)}, u32[]{:S(2)}) collective-permute-start(bf16[4,96,128]{2,1,0:T(8,128)(2,1)S(1)} %slice.12), channel_id=1, source_target_pairs={{0,8},{4,12},{8,0},{12,4},{1,9},{5,13},{9,1},{13,5},{2,10},{6,14},... | collective-permute-start | bytes 294920 | tf_op jit(solution)/shard_map/ppermute | solution.py:369
  48.7 5.9 %collective-permute-start.2 = (bf16[4,96,128]{2,1,0:T(8,128)(2,1)S(1)}, bf16[4,96,128]{2,1,0:T(8,128)(2,1)S(1)}, u32[]{:S(2)}, u32[]{:S(2)}) collective-permute-start(bf16[4,96,128]{2,1,0:T(8,128)(2,1)S(1)} %slice.12), channel_id=1, source_target_pairs={{0,12},{4,8},{8,4},{12,0},{1,13},{5,9},{9,5},{13,1},{2,14},{6,10},... | collective-permute-start | bytes 294920 | tf_op jit(solution)/shard_map/ppermute | solution.py:369
  58.3 11.4 %collective-permute-start.4 = (bf16[2,192,128]{2,1,0:T(8,128)(2,1)S(1)}, bf16[2,192,128]{2,1,0:T(8,128)(2,1)S(1)}, u32[]{:S(2)}, u32[]{:S(2)}) collective-permute-start(bf16[2,192,128]{2,1,0:T(8,128)(2,1)S(1)} %slice.16), channel_id=1, source_target_pairs={{0,64},{64,128},{128,192},{192,0},{1,65},{65,129},{129,193},{193,1... | collective-permute-start | bytes 294920 | tf_op jit(solution)/shard_map/ppermute | solution.py:374
  59.6 10.1 %collective-permute-start.6 = (bf16[2,192,128]{2,1,0:T(8,128)(2,1)S(1)}, bf16[2,192,128]{2,1,0:T(8,128)(2,1)S(1)}, u32[]{:S(2)}, u32[]{:S(2)}) collective-permute-start(bf16[2,192,128]{2,1,0:T(8,128)(2,1)S(1)} %slice.17), channel_id=1, source_target_pairs={{0,192},{64,0},{128,64},{192,128},{1,193},{65,1},{129,65},{193,129... | collective-permute-start | bytes 294920 | tf_op jit(solution)/shard_map/ppermute | solution.py:375
  69.7 14.4 %copy-start = (bf16[768,512]{1,0:T(8,128)(2,1)S(1)}, bf16[768,512]{1,0:T(8,128)(2,1)}, u32[]{:S(2)}) copy-start(bf16[768,512]{1,0:T(8,128)(2,1)} %get-tuple-element.16.mid_ref) | copy-start | bytes 2359300
  69.7 14.4 %copy-start.2 = (bf16[512,512]{1,0:T(8,128)(2,1)S(1)}, bf16[512,512]{1,0:T(8,128)(2,1)}, u32[]{:S(2)}) copy-start(bf16[512,512]{1,0:T(8,128)(2,1)} %w_ref.3) | copy-start | bytes 1572868
  69.7 14.4 %copy-start.5 = (f32[512]{0:T(512)S(1)}, f32[512]{0:T(512)}, u32[]{:S(2)}) copy-start(f32[512]{0:T(512)} %param.28) | copy-start | bytes 6148
  75.4 21.5 %copy-start.3 = (bf16[48,1024]{1,0:T(8,128)(2,1)S(1)}, bf16[48,1024]{1,0:T(8,128)(2,1)}, u32[]{:S(2)}) copy-start(bf16[48,1024]{1,0:T(8,128)(2,1)} %get-tuple-element.14.latmid_ref) | copy-start | bytes 294916
  75.4 21.5 %copy-start.4 = (f32[1024]{0:T(1024)S(1)}, f32[1024]{0:T(1024)}, u32[]{:S(2)}) copy-start(f32[1024]{0:T(1024)} %param.30) | copy-start | bytes 12292
  75.4 21.4 %all-to-all-start.1 = ((bf16[64,32,128]{2,1,0:T(8,128)(2,1)}), bf16[64,32,128]{2,1,0:T(8,128)(2,1)S(1)}, u32[]{:S(2)}, u32[]{:S(2)}) async-start(bf16[64,32,128]{2,1,0:T(8,128)(2,1)} %bitcast.5), calls=%async_computation.1 | async-start | bytes 1048576 | tf_op jit(solution)/shard_map/all_to_all | solution.py:413
Sparse Core Ops, SparseCore 0:
  40.7 31.3 all-gather.1

commit v3 on v2

--- a/solution.py
+++ b/solution.py
@@ -229,23 +229,27 @@
 
 
 def back_kernel(
-    got_ref, latmid_ref, gwlat_ref, mid_ref, query_ref, wo_hbm, wkv_hbm, tok_ref, lat_ref,
+    place_ref, got_ref, latmid_ref, gwlat_ref, mid_ref, query_ref, wo0, wo1, wo2, wo3, wkv_hbm,
+    tok_ref, lat_ref,
     wo, wkv, sems,
 ):
+    moves = [(source, wo.at[i]) for i, source in enumerate((wo0, wo1, wo2, wo3))]
     copies = [
         pltpu.make_async_copy(source, target, sems.at[i])
-        for i, (source, target) in enumerate(((wo_hbm, wo), (wkv_hbm, wkv)))
+        for i, (source, target) in enumerate(moves + [(wkv_hbm, wkv)])
     ]
     for copy in copies:
         copy.start()
+    me = place_ref[0]
     rows = latmid_ref.shape[0]
     half = rows // 2
     low = low_lanes(half)
     low8 = low_lanes(8)
-    heads = [None] * 16
-    for t in range(4):
-        for lat in range(4):
-            parts = [got_ref[t * 16 + x * 4 + lat].astype(f32) for x in range(4)]
+    latents = latmid_ref[...].astype(f32)
+    for d in range(4):
+        heads = []
+        for t in range(4):
+            parts = [got_ref[t * 16 + x * 4 + (me ^ d)].astype(f32) for x in range(4)]
             sizes = [
                 p[half:] + pltpu.roll(p[half:], 127, 1) + pltpu.roll(p[half:], 126, 1)
                 for p in parts
@@ -261,19 +265,18 @@
                     for b, c in ((b, 3 * (b + half // 8)) for b in range(half // 8))
                 ]
                 mixed = mixed + p[:half] * jnp.concatenate(spread, axis=0)
-            heads[lat * 4 + t] = mixed
-    pairs = []
-    for p in range(8):
-        one, two = heads[2 * p], heads[2 * p + 1]
-        top = jnp.where(low, one, swap(two))
-        end = jnp.where(low, swap(one), two)
-        pairs.append(jnp.concatenate([top, end], axis=0).astype(bf16))
-    mixed = jnp.concatenate(pairs, axis=1)
-    copies[0].wait()
-    latents = (latmid_ref[...].astype(f32) + dot(mixed, wo[...])).astype(bf16)
+            heads.append(mixed)
+        pairs = []
+        for one, two in ((heads[0], heads[1]), (heads[2], heads[3])):
+            top = jnp.where(low, one, swap(two))
+            end = jnp.where(low, swap(one), two)
+            pairs.append(jnp.concatenate([top, end], axis=0).astype(bf16))
+        copies[d].wait()
+        latents = latents + dot(jnp.concatenate(pairs, axis=1), wo[d])
+    latents = latents.astype(bf16)
     lat_ref[...] = latents
     normed = norm(latents.astype(f32), gwlat_ref[...])
-    copies[1].wait()
+    copies[4].wait()
     kv = dot(normed, wkv[...]).astype(bf16)
     head_of_row = lax.broadcasted_iota(jnp.int32, (8 * NLAT, 512), 0) // NLAT
     head_of_lane = lax.broadcasted_iota(jnp.int32, (8 * NLAT, 512), 1) // HEAD
@@ -325,6 +328,9 @@
     token_rows, width = tokens.shape
     lat_rows, lat_width = latents.shape
     row = lambda gain: gain.reshape(1, -1)
+    other = [(0, 1), (1, 0)]
+    w_o_core = lax.ppermute(w_o_glob, "core", other)
+    w_o_yh = lax.ppermute(w_o_glob, "yh", other)
     vmem = pl.BlockSpec(memory_space=pltpu.VMEM)
     hbm = pl.BlockSpec(memory_space=pl.ANY)
     weights = (w_qkv_tok, w_o_tok, w_kv_read, w_q_read)
@@ -362,8 +368,6 @@
         name="project",
     )(block, w_qkv_glob)
     own = lax.all_to_all(sent, HEADS4, 0, 0, tiled=True)
-    own, w_o_here = lax.optimization_barrier((own, w_o_glob))
-    w_o_all = lax.all_gather(w_o_here, LAT, axis=0, tiled=True)
     own_kv = own[:, :block_rows]
     own_q = own[:, block_rows:]
     others_q = [lax.ppermute(own_q, "x", [(i, i ^ k) for i in range(4)]) for k in (1, 2, 3)]
@@ -411,7 +415,8 @@
         name="attend_last",
     )(place, queries, kv_far1, kv_far2, state)
     got = lax.all_to_all(partial.reshape(64, message, 128), OUT64, 0, 0, tiled=True)
-    tokens_late, partial = lax.optimization_barrier((tokens_mid, partial))
+    tokens_late, w_o_late, partial = lax.optimization_barrier((tokens_mid, w_o_yh, partial))
+    w_o_both = lax.ppermute(w_o_late, "core", other)
     query = pl.pallas_call(
         write_query_kernel,
         in_specs=[vmem] * 3,
@@ -423,20 +428,32 @@
     )(tokens_late, row(gain_write), w_q_write)
     tokens_out, latents_out = pl.pallas_call(
         back_kernel,
-        in_specs=[vmem] * 5 + [hbm] * 2,
+        in_specs=[pl.BlockSpec(memory_space=pltpu.SMEM)] + [vmem] * 5 + [hbm] * 5,
         out_specs=[vmem] * 2,
         out_shape=[
             jax.ShapeDtypeStruct(tokens.shape, bf16),
             jax.ShapeDtypeStruct(latents.shape, bf16),
         ],
         scratch_shapes=[
-            pltpu.VMEM(w_o_all.shape, bf16),
+            pltpu.VMEM((4,) + w_o_glob.shape, bf16),
             pltpu.VMEM(w_kv_write.shape, bf16),
-            pltpu.SemaphoreType.DMA((2,)),
+            pltpu.SemaphoreType.DMA((5,)),
         ],
-        compiler_params=params(51),
+        compiler_params=params(49),
         name="back",
-    )(got, latents_mid, row(gain_wlat), tokens_late, query, w_o_all, w_kv_write)
+    )(
+        lax.axis_index(LAT).astype(jnp.int32).reshape(1),
+        got,
+        latents_mid,
+        row(gain_wlat),
+        tokens_late,
+        query,
+        w_o_glob,
+        w_o_core,
+        w_o_late,
+        w_o_both,
+        w_kv_write,
+    )
     return (tokens_out, latents_out)
 
 

time: 111 us -> 95.8 us (0.86)
  between operations: 14.2 us -> 0.95 us
  starting transfers between devices: 20.8 us -> 24 us
  waiting for transfers between devices: 17.7 us -> 14.5 us
  Pallas kernels: 38.4 us -> 36.3 us
    ppermute x0 -> x3, starting transfers between devices: none -> 3.24 us  [the longest x1 2.59 us: local(): w_o_yh = lax.ppermute(w_o_glob, 'yh', other)]
    ppermute x3, waiting for transfers between devices: 5.67 us -> 3.09 us  [local(): lax.ppermute(own_q, 'x', [(i, i ^ k) for i in range(4)])]
    all_to_all x1, waiting for transfers between devices: 12 us -> 9.53 us  [local(): lax.all_to_all(partial.reshape(64, message, 128), OUT64, 0, 0, tiled=True)]
    pallas_call x1, Pallas kernels: 7.03 us -> 4.97 us  [local(): pl.pallas_call(back_kernel, in_specs=[pl.BlockSpec(memory_space=pltpu.SME...]
    ppermute x0 -> x3, waiting for transfers between devices: none -> 1.86 us  [the longest x1 0.96 us: local(): w_o_both = lax.ppermute(w_o_late, 'core', other)]
  transfers between devices with their start and end apart: 9 -> 11, of which waited for: 3 -> 5; matrix products, arithmetic and copies ran while one was open for 0% -> 0% of each run, Pallas kernels for 16% -> 18%
where the time goes in v3:
time: 95.8 us; the launch traced here: 95.5 us
  Pallas kernels  36.3 us (38%)
  starting transfers between devices  24 us (25%)
  blocking collectives  19.7 us (21%)
  waiting for transfers between devices  14.5 us (15%)
    pallas_call x1, Pallas kernels, local(): pl.pallas_call(front_kernel, in_specs=[vmem] * 6 + [hbm] * 4, out_specs=[...  13.2 us
    all_gather x1, blocking collectives, local(): block = lax.all_gather(normed, LAT, axis=0, tiled=True)  11.1 us
    all_to_all x1, waiting for transfers between devices, local(): lax.all_to_all(partial.reshape(64, message, 128), OUT64, 0, 0, tiled=True)  9.53 us
    all_to_all x1, starting transfers between devices, local(): lax.all_to_all(partial.reshape(64, message, 128), OUT64, 0, 0, tiled=True)  8.71 us
    all_to_all x1, blocking collectives, local(): own = lax.all_to_all(sent, HEADS4, 0, 0, tiled=True)  8.59 us
    pallas_call x1, Pallas kernels, local(): pl.pallas_call(attend_next_kernel, in_specs=[vmem] * 4, out_specs=vmem, o...  7.68 us
    pallas_call x1, Pallas kernels, local(): pl.pallas_call(attend_last_kernel, in_specs=[pl.BlockSpec(memory_space=pl...  5.6 us
    pallas_call x1, Pallas kernels, local(): pl.pallas_call(back_kernel, in_specs=[pl.BlockSpec(memory_space=pltpu.SME...  4.97 us
  transfers between devices with their start and end apart: 11, of which 5 were waited for; matrix products, arithmetic and copies ran while one was open for 0% of the time, Pallas kernels for 18%

profile of v3, /device:TPU:1, one launch (start us, length us, event | category | flops | bytes accessed | tf_op | source)
XLA Modules:
  0.0 95.5 jit_solution(3226398940656814478)
XLA Ops:
  0.6 0.0 copy-start.1
  0.6 13.2 %front.1 = (bf16[768,512]{1,0:T(8,128)(2,1)}, bf16[48,1024]{1,0:T(8,128)(2,1)}, bf16[48,1024]{1,0:T(8,128)(2,1)}) custom-call(bf16[768,512]{1,0:T(8,128)(2,1)} %tok_ref.1, bf16[48,1024]{1,0:T(8,128)(2,1)} %lat_ref.1, f32[1,512]{1,0:T(1,128)} %bitcast.13, f32[1,512]{1,0:T(1,128)} %bitcast.14, f32[1,1024]{1,0:T(1,128)} %bitcast.11, f32[1,1024]{1,0:T(1,128)} %bitcast.12, ...), custom_call_target="tpu_custom_call" | custom-call | tf_op jit(solution)/shard_map/front/pallas_call | solution.py:337
  13.8 0.0 copy-start.3
  13.9 11.1 %all_gather.3.block_ref = bf16[192,1024]{1,0:T(8,128)(2,1)S(1)} all-gather(bf16[48,1024]{1,0:T(8,128)(2,1)} %get-tuple-element.9), channel_id=1, replica_groups=mesh['za'=2,'zb'=2,'zc'=2,'yl'=2,'x'=4,'yh'=2,'core'=2] {'yh','core'}, dimensions={0}, use_global_device_ids=true | all-gather | bytes 491520 | tf_op jit(solution)/shard_map/all_gather | solution.py:359
  24.9 0.0 copy-done.1
  24.9 0.6 project.1
  25.5 8.6 %all_to_all.10.own_ref = bf16[4,288,128]{2,1,0:T(8,128)(2,1)S(1)} all-to-all(bf16[4,288,128]{2,1,0:T(8,128)(2,1)S(1)} %project.1), channel_id=1, replica_groups=mesh['za'=2,'zb'=2,'zc'=2,'yl'=2,'x'=4,'yh'=2,'core'=2] {'zc','yl'}, dimensions={0} | all-to-all | bytes 589824 | tf_op jit(solution)/shard_map/all_to_all | solution.py:370
  34.1 2.1 %collective-permute-start.3 = (bf16[4,192,128]{2,1,0:T(8,128)(2,1)S(1)}, bf16[4,192,128]{2,1,0:T(8,128)(2,1)S(1)}, u32[]{:S(2)}, u32[]{:S(2)}) collective-permute-start(bf16[4,192,128]{2,1,0:T(8,128)(2,1)S(1)} %slice.17), channel_id=1, source_target_pairs={{0,64},{64,128},{128,192},{192,0},{1,65},{65,129},{129,193},{193,1... | collective-permute-start | bytes 589832 | tf_op jit(solution)/shard_map/ppermute | solution.py:376
  36.2 2.3 %collective-permute-start.5 = (bf16[4,192,128]{2,1,0:T(8,128)(2,1)S(1)}, bf16[4,192,128]{2,1,0:T(8,128)(2,1)S(1)}, u32[]{:S(2)}, u32[]{:S(2)}) collective-permute-start(bf16[4,192,128]{2,1,0:T(8,128)(2,1)S(1)} %slice.17), channel_id=1, source_target_pairs={{0,192},{64,0},{128,64},{192,128},{1,193},{65,1},{129,65},{193,129... | collective-permute-start | bytes 589832 | tf_op jit(solution)/shard_map/ppermute | solution.py:377
  38.5 1.3 %collective-permute-start = (bf16[4,96,128]{2,1,0:T(8,128)(2,1)S(1)}, bf16[4,96,128]{2,1,0:T(8,128)(2,1)S(1)}, u32[]{:S(2)}, u32[]{:S(2)}) collective-permute-start(bf16[4,96,128]{2,1,0:T(8,128)(2,1)S(1)} %slice.16), channel_id=1, source_target_pairs={{0,4},{4,0},{8,12},{12,8},{1,5},{5,1},{9,13},{13,9},{2,6},{6,2},{1... | collective-permute-start | bytes 294920 | tf_op jit(solution)/shard_map/ppermute | solution.py:373
  39.8 2.5 %collective-permute-start.1 = (bf16[4,96,128]{2,1,0:T(8,128)(2,1)S(1)}, bf16[4,96,128]{2,1,0:T(8,128)(2,1)S(1)}, u32[]{:S(2)}, u32[]{:S(2)}) collective-permute-start(bf16[4,96,128]{2,1,0:T(8,128)(2,1)S(1)} %slice.16), channel_id=1, source_target_pairs={{0,8},{4,12},{8,0},{12,4},{1,9},{5,13},{9,1},{13,5},{2,10},{6,14},... | collective-permute-start | bytes 294920 | tf_op jit(solution)/shard_map/ppermute | solution.py:373
  42.3 0.2 collective-permute-start.2
  42.5 0.0 collective-permute-done.q1_ref
  42.5 0.0 copy-done.3
  42.5 2.6 %collective-permute-start.7 = (bf16[256,1024]{1,0:T(8,128)(2,1)S(1)}, bf16[256,1024]{1,0:T(8,128)(2,1)}, u32[]{:S(2)}, u32[]{:S(2)}) collective-permute-start(bf16[256,1024]{1,0:T(8,128)(2,1)S(1)} %copy-done.3), channel_id=1, source_target_pairs={{0,2},{2,0},{1,3},{3,1},{4,6},{6,4},{5,7},{7,5},{8,10},{10,8},{9,1... | collective-permute-start | bytes 1572872 | tf_op jit(solution)/shard_map/ppermute | solution.py:333
  45.1 0.3 collective-permute-done.1.q2_ref
  45.3 2.8 %collective-permute-done.2.q3_ref = bf16[4,96,128]{2,1,0:T(8,128)(2,1)S(1)} collective-permute-done((bf16[4,96,128]{2,1,0:T(8,128)(2,1)S(1)}, bf16[4,96,128]{2,1,0:T(8,128)(2,1)S(1)}, u32[]{:S(2)}, u32[]{:S(2)}) %collective-permute-start.2) | collective-permute-done | bytes 98336 | tf_op jit(solution)/shard_map/ppermute | solution.py:373
  48.1 3.7 %attend_first.1 = (bf16[3072,128]{1,0:T(8,128)(2,1)S(1)}, f32[2,3072,128]{2,1,0:T(8,128)S(1)}) custom-call(bf16[4,288,128]{2,1,0:T(8,128)(2,1)S(1)} %all_to_all.10.own_ref, bf16[4,96,128]{2,1,0:T(8,128)(2,1)S(1)} %collective-permute-done.q1_ref, bf16[4,96,128]{2,1,0:T(8,128)(2,1)S(1)} %collective-permute-done.1.q2_ref, ...), custom_call_target="tpu_custom_call" | custom-call | flops 603979776 | bytes 3932160 | tf_op jit(solution)/shard_map/attend_first/pallas_call | solution.py:386
  51.8 0.0 collective-permute-done.3.kv1_ref
  51.8 1.3 %collective-permute-start.4 = (bf16[2,192,128]{2,1,0:T(8,128)(2,1)S(1)}, bf16[2,192,128]{2,1,0:T(8,128)(2,1)S(1)}, u32[]{:S(2)}, u32[]{:S(2)}) collective-permute-start(bf16[2,192,128]{2,1,0:T(8,128)(2,1)S(1)} %slice.18), channel_id=1, source_target_pairs={{0,64},{64,128},{128,192},{192,0},{1,65},{65,129},{129,193},{193,1... | collective-permute-start | bytes 294920 | tf_op jit(solution)/shard_map/ppermute | solution.py:378
  53.1 0.0 collective-permute-done.5.kv2_ref
  53.2 2.4 %collective-permute-start.6 = (bf16[2,192,128]{2,1,0:T(8,128)(2,1)S(1)}, bf16[2,192,128]{2,1,0:T(8,128)(2,1)S(1)}, u32[]{:S(2)}, u32[]{:S(2)}) collective-permute-start(bf16[2,192,128]{2,1,0:T(8,128)(2,1)S(1)} %slice.19), channel_id=1, source_target_pairs={{0,192},{64,0},{128,64},{192,128},{1,193},{65,1},{129,65},{193,129... | collective-permute-start | bytes 294920 | tf_op jit(solution)/shard_map/ppermute | solution.py:379
  55.6 7.7 %attend_next.1.before_ref = f32[2,3072,128]{2,1,0:T(8,128)S(1)} custom-call(bf16[3072,128]{1,0:T(8,128)(2,1)S(1)} %get-tuple-element.10.queries_ref, bf16[4,192,128]{2,1,0:T(8,128)(2,1)S(1)} %collective-permute-done.3.kv1_ref, bf16[4,192,128]{2,1,0:T(8,128)(2,1)S(1)} %collective-permute-done.5.kv2_ref, f32[2,3072,128]{2,1,0:T(8,128)S(1)} %get-tuple-element.11.before_ref), custom_call_target="tpu_custom_call" | custom-call | flops 1207959552 | bytes 3932160 | tf_op jit(solution)/shard_map/attend_next/pallas_call | solution.py:398
  63.3 0.0 collective-permute-done.4.kv1_ref
  63.3 0.0 collective-permute-done.6.kv2_ref
  63.3 0.0 copy-start
  63.3 0.0 copy-start.2
  63.3 0.0 copy-start.6
  63.3 5.6 %attend_last.1 = bf16[4,4,128,128]{3,2,1,0:T(8,128)(2,1)} custom-call(s32[1]{0:T(128)} %bitcast.1.place_ref, bf16[3072,128]{1,0:T(8,128)(2,1)S(1)} %get-tuple-element.10.queries_ref, bf16[2,192,128]{2,1,0:T(8,128)(2,1)S(1)} %collective-permute-done.4.kv1_ref, bf16[2,192,128]{2,1,0:T(8,128)(2,1)S(1)} %collective-permute-done.6.kv2_ref, ...), custom_call_target="tpu_custom_call" | custom-call | flops 603979776 | bytes 3932160 | tf_op jit(solution)/shard_map/attend_last/pallas_call | solution.py:408
  68.9 0.0 copy-start.4
  68.9 0.0 copy-start.5
  68.9 8.7 %all-to-all-start.1 = ((bf16[64,32,128]{2,1,0:T(8,128)(2,1)}), bf16[64,32,128]{2,1,0:T(8,128)(2,1)S(1)}, u32[]{:S(2)}, u32[]{:S(2)}) async-start(bf16[64,32,128]{2,1,0:T(8,128)(2,1)} %bitcast.6), calls=%async_computation.1 | async-start | bytes 1048576 | tf_op jit(solution)/shard_map/all_to_all | solution.py:417
  77.6 0.5 collective-permute-start.8
  78.2 0.0 collective-permute-done.7.wo2
  78.2 0.1 collective-permute-start.9
  78.3 0.0 copy-done
  78.3 0.0 copy-done.2
  78.3 0.0 copy-done.6
  78.3 0.6 write_query.1.query_ref
  79.0 0.9 collective-permute-done.8.wo1
  79.9 1.0 %collective-permute-done.9.wo3 = bf16[256,1024]{1,0:T(8,128)(2,1)} collective-permute-done((bf16[256,1024]{1,0:T(8,128)(2,1)}, bf16[256,1024]{1,0:T(8,128)(2,1)}, u32[]{:S(2)}, u32[]{:S(2)}) %collective-permute-start.9) | collective-permute-done | bytes 524320 | tf_op jit(solution)/shard_map/ppermute | solution.py:419
  80.8 9.5 %all-to-all-done.1.got_ref = bf16[64,32,128]{2,1,0:T(8,128)(2,1)S(1)} async-done(((bf16[64,32,128]{2,1,0:T(8,128)(2,1)}), bf16[64,32,128]{2,1,0:T(8,128)(2,1)S(1)}, u32[]{:S(2)}, u32[]{:S(2)}) %all-to-all-start.1) | async-done | bytes 524320 | tf_op jit(solution)/shard_map/all_to_all | solution.py:417
  90.3 0.0 copy-done.4
  90.4 0.0 copy-done.5
  90.4 5.0 %back.1 = (bf16[768,512]{1,0:T(8,128)(2,1)}, bf16[48,1024]{1,0:T(8,128)(2,1)}) custom-call(s32[1]{0:T(128)} %bitcast.place_ref, bf16[64,32,128]{2,1,0:T(8,128)(2,1)S(1)} %all-to-all-done.1.got_ref, bf16[48,1024]{1,0:T(8,128)(2,1)S(1)} %copy-done.4, f32[1,1024]{1,0:T(1,128)S(1)} %bitcast.9, bf16[768,512]{1,0:T(8,128)(2,1)S(1)} %copy-done, ...), custom_call_target="tpu_custom_call" | custom-call | tf_op jit(solution)/shard_map/back/pallas_call | solution.py:429
  (4 shorter events, 0.0 us)
Async XLA Ops:
  0.6 24.3 %copy-start.1 = (bf16[3,1024,256]{2,1,0:T(8,128)(2,1)S(1)}, bf16[3,1024,256]{2,1,0:T(8,128)(2,1)}, u32[]{:S(2)}) copy-start(bf16[3,1024,256]{2,1,0:T(8,128)(2,1)} %w_ref.2) | copy-start | bytes 4718596
  13.8 28.6 %copy-start.3 = (bf16[256,1024]{1,0:T(8,128)(2,1)S(1)}, bf16[256,1024]{1,0:T(8,128)(2,1)}, u32[]{:S(2)}) copy-start(bf16[256,1024]{1,0:T(8,128)(2,1)} %wo0.1) | copy-start | bytes 1572868
  34.1 17.7 %collective-permute-start.3 = (bf16[4,192,128]{2,1,0:T(8,128)(2,1)S(1)}, bf16[4,192,128]{2,1,0:T(8,128)(2,1)S(1)}, u32[]{:S(2)}, u32[]{:S(2)}) collective-permute-start(bf16[4,192,128]{2,1,0:T(8,128)(2,1)S(1)} %slice.17), channel_id=1, source_target_pairs={{0,64},{64,128},{128,192},{192,0},{1,65},{65,129},{129,193},{193,1... | collective-permute-start | bytes 589832 | tf_op jit(solution)/shard_map/ppermute | solution.py:376
  36.2 17.0 %collective-permute-start.5 = (bf16[4,192,128]{2,1,0:T(8,128)(2,1)S(1)}, bf16[4,192,128]{2,1,0:T(8,128)(2,1)S(1)}, u32[]{:S(2)}, u32[]{:S(2)}) collective-permute-start(bf16[4,192,128]{2,1,0:T(8,128)(2,1)S(1)} %slice.17), channel_id=1, source_target_pairs={{0,192},{64,0},{128,64},{192,128},{1,193},{65,1},{129,65},{193,129... | collective-permute-start | bytes 589832 | tf_op jit(solution)/shard_map/ppermute | solution.py:377
  38.5 3.9 %collective-permute-start = (bf16[4,96,128]{2,1,0:T(8,128)(2,1)S(1)}, bf16[4,96,128]{2,1,0:T(8,128)(2,1)S(1)}, u32[]{:S(2)}, u32[]{:S(2)}) collective-permute-start(bf16[4,96,128]{2,1,0:T(8,128)(2,1)S(1)} %slice.16), channel_id=1, source_target_pairs={{0,4},{4,0},{8,12},{12,8},{1,5},{5,1},{9,13},{13,9},{2,6},{6,2},{1... | collective-permute-start | bytes 294920 | tf_op jit(solution)/shard_map/ppermute | solution.py:373
  39.8 5.5 %collective-permute-start.1 = (bf16[4,96,128]{2,1,0:T(8,128)(2,1)S(1)}, bf16[4,96,128]{2,1,0:T(8,128)(2,1)S(1)}, u32[]{:S(2)}, u32[]{:S(2)}) collective-permute-start(bf16[4,96,128]{2,1,0:T(8,128)(2,1)S(1)} %slice.16), channel_id=1, source_target_pairs={{0,8},{4,12},{8,0},{12,4},{1,9},{5,13},{9,1},{13,5},{2,10},{6,14},... | collective-permute-start | bytes 294920 | tf_op jit(solution)/shard_map/ppermute | solution.py:373
  42.3 5.9 %collective-permute-start.2 = (bf16[4,96,128]{2,1,0:T(8,128)(2,1)S(1)}, bf16[4,96,128]{2,1,0:T(8,128)(2,1)S(1)}, u32[]{:S(2)}, u32[]{:S(2)}) collective-permute-start(bf16[4,96,128]{2,1,0:T(8,128)(2,1)S(1)} %slice.16), channel_id=1, source_target_pairs={{0,12},{4,8},{8,4},{12,0},{1,13},{5,9},{9,5},{13,1},{2,14},{6,10},... | collective-permute-start | bytes 294920 | tf_op jit(solution)/shard_map/ppermute | solution.py:373
  42.5 35.7 %collective-permute-start.7 = (bf16[256,1024]{1,0:T(8,128)(2,1)S(1)}, bf16[256,1024]{1,0:T(8,128)(2,1)}, u32[]{:S(2)}, u32[]{:S(2)}) collective-permute-start(bf16[256,1024]{1,0:T(8,128)(2,1)S(1)} %copy-done.3), channel_id=1, source_target_pairs={{0,2},{2,0},{1,3},{3,1},{4,6},{6,4},{5,7},{7,5},{8,10},{10,8},{9,1... | collective-permute-start | bytes 1572872 | tf_op jit(solution)/shard_map/ppermute | solution.py:333
  51.8 11.4 %collective-permute-start.4 = (bf16[2,192,128]{2,1,0:T(8,128)(2,1)S(1)}, bf16[2,192,128]{2,1,0:T(8,128)(2,1)S(1)}, u32[]{:S(2)}, u32[]{:S(2)}) collective-permute-start(bf16[2,192,128]{2,1,0:T(8,128)(2,1)S(1)} %slice.18), channel_id=1, source_target_pairs={{0,64},{64,128},{128,192},{192,0},{1,65},{65,129},{129,193},{193,1... | collective-permute-start | bytes 294920 | tf_op jit(solution)/shard_map/ppermute | solution.py:378
  53.2 10.1 %collective-permute-start.6 = (bf16[2,192,128]{2,1,0:T(8,128)(2,1)S(1)}, bf16[2,192,128]{2,1,0:T(8,128)(2,1)S(1)}, u32[]{:S(2)}, u32[]{:S(2)}) collective-permute-start(bf16[2,192,128]{2,1,0:T(8,128)(2,1)S(1)} %slice.19), channel_id=1, source_target_pairs={{0,192},{64,0},{128,64},{192,128},{1,193},{65,1},{129,65},{193,129... | collective-permute-start | bytes 294920 | tf_op jit(solution)/shard_map/ppermute | solution.py:379
  63.3 15.0 %copy-start = (bf16[768,512]{1,0:T(8,128)(2,1)S(1)}, bf16[768,512]{1,0:T(8,128)(2,1)}, u32[]{:S(2)}) copy-start(bf16[768,512]{1,0:T(8,128)(2,1)} %get-tuple-element.14.mid_ref) | copy-start | bytes 2359300
  63.3 15.0 %copy-start.2 = (bf16[512,512]{1,0:T(8,128)(2,1)S(1)}, bf16[512,512]{1,0:T(8,128)(2,1)}, u32[]{:S(2)}) copy-start(bf16[512,512]{1,0:T(8,128)(2,1)} %w_ref.3) | copy-start | bytes 1572868
  63.3 15.0 %copy-start.6 = (f32[512]{0:T(512)S(1)}, f32[512]{0:T(512)}, u32[]{:S(2)}) copy-start(f32[512]{0:T(512)} %param.28) | copy-start | bytes 6148
  68.9 21.4 %copy-start.4 = (bf16[48,1024]{1,0:T(8,128)(2,1)S(1)}, bf16[48,1024]{1,0:T(8,128)(2,1)}, u32[]{:S(2)}) copy-start(bf16[48,1024]{1,0:T(8,128)(2,1)} %get-tuple-element.12.latmid_ref) | copy-start | bytes 294916
  68.9 21.4 %copy-start.5 = (f32[1024]{0:T(1024)S(1)}, f32[1024]{0:T(1024)}, u32[]{:S(2)}) copy-start(f32[1024]{0:T(1024)} %param.30) | copy-start | bytes 12292
  68.9 21.4 %all-to-all-start.1 = ((bf16[64,32,128]{2,1,0:T(8,128)(2,1)}), bf16[64,32,128]{2,1,0:T(8,128)(2,1)S(1)}, u32[]{:S(2)}, u32[]{:S(2)}) async-start(bf16[64,32,128]{2,1,0:T(8,128)(2,1)} %bitcast.6), calls=%async_computation.1 | async-start | bytes 1048576 | tf_op jit(solution)/shard_map/all_to_all | solution.py:417
  77.6 2.2 %collective-permute-start.8 = (bf16[256,1024]{1,0:T(8,128)(2,1)S(1)}, bf16[256,1024]{1,0:T(8,128)(2,1)}, u32[]{:S(2)}, u32[]{:S(2)}) collective-permute-start(bf16[256,1024]{1,0:T(8,128)(2,1)S(1)} %copy-done.3), channel_id=1, source_target_pairs={{0,1},{1,0},{2,3},{3,2},{4,5},{5,4},{6,7},{7,6},{8,9},{9,8},{10,11... | collective-permute-start | bytes 1572872 | tf_op jit(solution)/shard_map/ppermute | solution.py:332
  78.2 2.6 %collective-permute-start.9 = (bf16[256,1024]{1,0:T(8,128)(2,1)}, bf16[256,1024]{1,0:T(8,128)(2,1)}, u32[]{:S(2)}, u32[]{:S(2)}) collective-permute-start(bf16[256,1024]{1,0:T(8,128)(2,1)} %collective-permute-done.7.wo2), channel_id=1, source_target_pairs={{0,1},{1,0},{2,3},{3,2},{4,5},{5,4},{6,7},{7,6},{8,9},{9,8},{10,11... | collective-permute-start | bytes 1572872 | tf_op jit(solution)/shard_map/ppermute | solution.py:419

commit v4 on v3

--- a/solution.py
+++ b/solution.py
@@ -11,6 +11,7 @@
 
 HEAD = 64
 G = 256
+TILE = 384
 NLAT = 16
 LOG2E = 1.4426950408889634
 SCALE = LOG2E * HEAD ** (-0.5)
@@ -67,6 +68,7 @@
     packed[...] = dot(normed, wqkv[...]).astype(bf16)
     low = low_lanes(G)
     zero = jnp.zeros((G, 128), bf16)
+    one = jnp.ones((G, 128), bf16)
     for g in range(groups):
         rows = slice(g * G, (g + 1) * G)
         for p in range(4):
@@ -76,7 +78,8 @@
             both = jnp.concatenate([jnp.where(low, q2, zero), jnp.where(low, zero, q2)], axis=0)
             s = dot_t(both, k2) * SCALE
             w = jnp.exp2(s - jnp.max(s, axis=-1, keepdims=True))
-            r = dot(w.astype(bf16), v2) / jnp.sum(w, axis=-1, keepdims=True)
+            r = dot(w.astype(bf16), jnp.concatenate([v2, one], axis=1))
+            r = r[:, :128] / r[:, 128:]
             mixed[rows, p * 128 : (p + 1) * 128] = jnp.where(low, r[:G], r[G:]).astype(bf16)
     copies[1].wait()
     mid = (x + dot(mixed[...], wo[...])).astype(bf16)
@@ -88,27 +91,34 @@
     copies[3].wait()
     kv[...] = dot(normed, wkv[...]).astype(bf16)
     part = lax.broadcasted_iota(jnp.int32, (NLAT, 256), 1) // HEAD
+    scores = []
     for g in range(groups):
-        rows = slice(g * G, (g + 1) * G)
-        mine = slice(g * NLAT, (g + 1) * NLAT)
-        blocks = []
         for quad in range(4):
-            q4 = query[mine, quad * 256 : (quad + 1) * 256]
-            k4 = kv[rows, quad * 256 : (quad + 1) * 256]
-            v4 = kv[rows, 1024 + quad * 256 : 1024 + (quad + 1) * 256]
+            lanes = slice(quad * 256, (quad + 1) * 256)
+            q4 = query[g * NLAT : (g + 1) * NLAT, lanes]
             stacked = jnp.concatenate(
                 [jnp.where(part == a, q4, jnp.zeros_like(q4)) for a in range(4)], axis=0
             )
-            s = dot_t(stacked, k4) * SCALE
-            w = jnp.exp2(s - jnp.max(s, axis=-1, keepdims=True))
-            r = dot(w.astype(bf16), v4) / jnp.sum(w, axis=-1, keepdims=True)
+            scores.append(dot_t(stacked, kv[g * G : (g + 1) * G, lanes]))
+    s = jnp.concatenate(scores, axis=0) * SCALE
+    w = jnp.exp2(s - jnp.max(s, axis=-1, keepdims=True))
+    total = jnp.sum(w, axis=-1, keepdims=True)
+    w = w.astype(bf16)
+    reads = []
+    for g in range(groups):
+        blocks = []
+        for quad in range(4):
+            at = slice((g * 4 + quad) * 4 * NLAT, (g * 4 + quad + 1) * 4 * NLAT)
+            lanes = slice(1024 + quad * 256, 1024 + (quad + 1) * 256)
+            r = dot(w[at], kv[g * G : (g + 1) * G, lanes]) / total[at]
             got = jnp.zeros((NLAT, 256), f32)
             for a in range(4):
                 got = jnp.where(part == a, r[a * NLAT : (a + 1) * NLAT], got)
             blocks.append(got)
-        latmid = (lat[mine] + jnp.concatenate(blocks, axis=1)).astype(bf16)
-        latmid_ref[mine, :] = latmid
-        normed_ref[mine, :] = norm(latmid.astype(f32), gglob_ref[...])
+        reads.append(jnp.concatenate(blocks, axis=1))
+    latmid = (lat + jnp.concatenate(reads, axis=0)).astype(bf16)
+    latmid_ref[...] = latmid
+    normed_ref[...] = norm(latmid.astype(f32), gglob_ref[...])
 
 
 def project_kernel(block_ref, w_ref, out_ref):
@@ -148,8 +158,8 @@
         [ref[t, :rows] for ref in key_refs for t in range(ref.shape[0])], axis=0
     )
     values = jnp.where(low_lanes(keys.shape[0]), jnp.ones_like(keys), keys)
-    step = 4 * rows
-    for k in range(4):
+    step = TILE
+    for k in range(queries.shape[0] // step):
         at = slice(k * step, (k + 1) * step)
         s = dot_t(queries[at, :], keys) * SCALE
         peak = jnp.max(s, axis=-1, keepdims=True)
@@ -164,10 +174,10 @@
         finish(k, state, peak)
 
 
-def keep_state(state_ref, step):
+def keep_state(state_ref):
     def keep(k, state, peak):
-        state_ref[0, k * step : (k + 1) * step, :] = state
-        state_ref[1, k * step : (k + 1) * step, :] = jnp.broadcast_to(peak, state.shape)
+        state_ref[0, k * TILE : (k + 1) * TILE, :] = state
+        state_ref[1, k * TILE : (k + 1) * TILE, :] = jnp.broadcast_to(peak, state.shape)
 
     return keep
 
@@ -175,13 +185,13 @@
 def attend_first_kernel(own_ref, q1_ref, q2_ref, q3_ref, queries_ref, state_ref):
     rows = q1_ref.shape[1] * 2
     unpack_queries((own_ref, q1_ref, q2_ref, q3_ref), (rows, 0, 0, 0), rows, queries_ref)
-    attend_part(queries_ref, (own_ref,), rows, None, keep_state(state_ref, 4 * rows))
+    attend_part(queries_ref, (own_ref,), rows, None, keep_state(state_ref))
 
 
 def attend_next_kernel(queries_ref, kv1_ref, kv2_ref, before_ref, state_ref):
     rows = kv1_ref.shape[1]
     attend_part(
-        queries_ref, (kv1_ref, kv2_ref), rows, before_ref, keep_state(state_ref, 4 * rows)
+        queries_ref, (kv1_ref, kv2_ref), rows, before_ref, keep_state(state_ref)
     )
 
 
@@ -196,7 +206,7 @@
 
     def send(k, state, peak):
         turned = swap(state)
-        for t in range(4):
+        for t in range(TILE // rows):
             for u in range(4):
                 at = (t * 4 + u) * unit
                 top = slice(at, at + half)
@@ -217,7 +227,8 @@
                 stats = jnp.where(
                     term == 0, first, jnp.where(term == 1, second, size - first - second)
                 )
-                out_ref[t, me ^ k, u * 32 : (u + 1) * 32] = jnp.concatenate(
+                source = k * (TILE // rows) + t
+                out_ref[source % 4, me ^ (source // 4), u * 32 : (u + 1) * 32] = jnp.concatenate(
                     [packed, stats], axis=0
                 ).astype(bf16)
 
@@ -231,7 +242,7 @@
 def back_kernel(
     place_ref, got_ref, latmid_ref, gwlat_ref, mid_ref, query_ref, wo0, wo1, wo2, wo3, wkv_hbm,
     tok_ref, lat_ref,
-    wo, wkv, sems,
+    wo, wkv, shares, sems,
 ):
     moves = [(source, wo.at[i]) for i, source in enumerate((wo0, wo1, wo2, wo3))]
     copies = [
@@ -245,26 +256,26 @@
     half = rows // 2
     low = low_lanes(half)
     low8 = low_lanes(8)
+    stats = got_ref[:, half:].astype(f32).reshape(64 * 8, 128)
+    sizes = stats + pltpu.roll(stats, 127, 1) + pltpu.roll(stats, 126, 1)
+    sizes = sizes.reshape(4, 4, 4, 8, 128)
+    weights = jnp.exp2(sizes - jnp.max(sizes, axis=1, keepdims=True))
+    weights = weights / jnp.sum(weights, axis=1, keepdims=True)
+    shares[...] = weights.reshape(64, 8, 128)
     latents = latmid_ref[...].astype(f32)
     for d in range(4):
         heads = []
         for t in range(4):
-            parts = [got_ref[t * 16 + x * 4 + (me ^ d)].astype(f32) for x in range(4)]
-            sizes = [
-                p[half:] + pltpu.roll(p[half:], 127, 1) + pltpu.roll(p[half:], 126, 1)
-                for p in parts
-            ]
-            peak = functools.reduce(jnp.maximum, sizes)
-            weights = [jnp.exp2(s - peak) for s in sizes]
-            total = functools.reduce(lax.add, weights)
             mixed = jnp.zeros((half, 128), f32)
-            for p, w in zip(parts, weights):
-                share = w / total
+            for x in range(4):
+                source = t * 16 + x * 4 + (me ^ d)
+                share = shares[source]
                 spread = [
                     jnp.where(low8, share[:, 3 * b : 3 * b + 1], share[:, c : c + 1])
                     for b, c in ((b, 3 * (b + half // 8)) for b in range(half // 8))
                 ]
-                mixed = mixed + p[:half] * jnp.concatenate(spread, axis=0)
+                part = got_ref[source].astype(f32)[:half]
+                mixed = mixed + part * jnp.concatenate(spread, axis=0)
             heads.append(mixed)
         pairs = []
         for one, two in ((heads[0], heads[1]), (heads[2], heads[3])):
@@ -282,19 +293,25 @@
     head_of_lane = lax.broadcasted_iota(jnp.int32, (8 * NLAT, 512), 1) // HEAD
     here = head_of_row == head_of_lane
     ones = jnp.where(here, 1.0, 0.0).astype(bf16)
-    for g in range(rows // NLAT):
-        mid = mid_ref[g * G : (g + 1) * G, :].astype(f32)
-        query = query_ref[g * G : (g + 1) * G, :]
+    groups = rows // NLAT
+    zero = jnp.zeros((8 * NLAT, 512), bf16)
+    scores, values = [], []
+    for g in range(groups):
         k = kv[g * NLAT : (g + 1) * NLAT, :512]
         v = kv[g * NLAT : (g + 1) * NLAT, 512:]
-        zero = jnp.zeros((8 * NLAT, 512), bf16)
         k8 = jnp.where(here, jnp.concatenate([k] * 8, axis=0), zero)
         v8 = jnp.where(here, jnp.concatenate([v] * 8, axis=0), zero)
-        s = (dot_t(k8, query) * SCALE).reshape(8, NLAT, G)
-        w = jnp.exp2(s - jnp.max(s, axis=1, keepdims=True)).reshape(8 * NLAT, G).astype(bf16)
-        turned = w.T
-        written = dot(turned, v8) / dot(turned, ones)
-        tok_ref[g * G : (g + 1) * G, :] = (mid + written).astype(bf16)
+        values.append(jnp.concatenate([v8, ones], axis=1))
+        scores.append(dot_t(k8, query_ref[g * G : (g + 1) * G, :]))
+    s = (jnp.concatenate(scores, axis=1) * SCALE).reshape(8, NLAT, groups * G)
+    w = jnp.exp2(s - jnp.max(s, axis=1, keepdims=True)).reshape(8 * NLAT, groups * G)
+    turned = w.astype(bf16).T
+    for g in range(groups):
+        at = slice(g * G, (g + 1) * G)
+        written = dot(turned[at], values[g])
+        tok_ref[at, :] = (
+            mid_ref[at, :].astype(f32) + written[:, :512] / written[:, 512:]
+        ).astype(bf16)
 
 
 def params(megabytes):
@@ -437,6 +454,7 @@
         scratch_shapes=[
             pltpu.VMEM((4,) + w_o_glob.shape, bf16),
             pltpu.VMEM(w_kv_write.shape, bf16),
+            pltpu.VMEM((64, 8, 128), f32),
             pltpu.SemaphoreType.DMA((5,)),
         ],
         compiler_params=params(49),

time: 95.8 us -> 90.9 us (0.949)
  Pallas kernels: 36.3 us -> 31.6 us
    pallas_call x1, Pallas kernels: 13.2 us -> 10.8 us  [local(): pl.pallas_call(front_kernel, in_specs=[vmem] * 6 + [hbm] * 4, out_specs=[...]
  transfers between devices with their start and end apart: 11 -> 11, of which waited for: 5 -> 5; matrix products, arithmetic and copies ran while one was open for 0% -> 0% of each run, Pallas kernels for 18% -> 17%
where the time goes in v4:
time: 90.9 us; the launch traced here: 90.6 us
  Pallas kernels  31.6 us (35%)
  starting transfers between devices  24 us (26%)
  blocking collectives  19.7 us (22%)
  waiting for transfers between devices  14.3 us (16%)
  between operations  0.95 us (1%)
    all_gather x1, blocking collectives, local(): block = lax.all_gather(normed, LAT, axis=0, tiled=True)  11.1 us
    pallas_call x1, Pallas kernels, local(): pl.pallas_call(front_kernel, in_specs=[vmem] * 6 + [hbm] * 4, out_specs=[...  10.8 us
    all_to_all x1, waiting for transfers between devices, local(): lax.all_to_all(partial.reshape(64, message, 128), OUT64, 0, 0, tiled=True)  9.53 us
    all_to_all x1, blocking collectives, local(): own = lax.all_to_all(sent, HEADS4, 0, 0, tiled=True)  8.59 us
    all_to_all x1, starting transfers between devices, local(): lax.all_to_all(partial.reshape(64, message, 128), OUT64, 0, 0, tiled=True)  8.49 us
    pallas_call x1, Pallas kernels, local(): pl.pallas_call(attend_next_kernel, in_specs=[vmem] * 4, out_specs=vmem, o...  6.77 us
    pallas_call x1, Pallas kernels, local(): pl.pallas_call(attend_last_kernel, in_specs=[pl.BlockSpec(memory_space=pl...  4.82 us
    pallas_call x1, Pallas kernels, local(): pl.pallas_call(back_kernel, in_specs=[pl.BlockSpec(memory_space=pltpu.SME...  4.46 us
  transfers between devices with their start and end apart: 11, of which 5 were waited for; matrix products, arithmetic and copies ran while one was open for 0% of the time, Pallas kernels for 17%

profile of v4, /device:TPU:1, one launch (start us, length us, event | category | flops | bytes accessed | tf_op | source)
XLA Modules:
  0.0 90.6 jit_solution(11484878175961918473)
XLA Ops:
  0.6 0.0 copy-start.1
  0.6 10.8 %front.1 = (bf16[768,512]{1,0:T(8,128)(2,1)}, bf16[48,1024]{1,0:T(8,128)(2,1)}, bf16[48,1024]{1,0:T(8,128)(2,1)}) custom-call(bf16[768,512]{1,0:T(8,128)(2,1)} %tok_ref.1, bf16[48,1024]{1,0:T(8,128)(2,1)} %lat_ref.1, f32[1,512]{1,0:T(1,128)} %bitcast.13, f32[1,512]{1,0:T(1,128)} %bitcast.14, f32[1,1024]{1,0:T(1,128)} %bitcast.11, f32[1,1024]{1,0:T(1,128)} %bitcast.12, ...), custom_call_target="tpu_custom_call" | custom-call | tf_op jit(solution)/shard_map/front/pallas_call | solution.py:354
  11.5 0.0 copy-start.3
  11.5 11.1 %all_gather.3.block_ref = bf16[192,1024]{1,0:T(8,128)(2,1)S(1)} all-gather(bf16[48,1024]{1,0:T(8,128)(2,1)} %get-tuple-element.9), channel_id=1, replica_groups=mesh['za'=2,'zb'=2,'zc'=2,'yl'=2,'x'=4,'yh'=2,'core'=2] {'yh','core'}, dimensions={0}, use_global_device_ids=true | all-gather | bytes 491520 | tf_op jit(solution)/shard_map/all_gather | solution.py:376
  22.5 0.0 copy-done.1
  22.5 0.6 project.1
  23.1 8.6 %all_to_all.10.own_ref = bf16[4,288,128]{2,1,0:T(8,128)(2,1)S(1)} all-to-all(bf16[4,288,128]{2,1,0:T(8,128)(2,1)S(1)} %project.1), channel_id=1, replica_groups=mesh['za'=2,'zb'=2,'zc'=2,'yl'=2,'x'=4,'yh'=2,'core'=2] {'zc','yl'}, dimensions={0} | all-to-all | bytes 589824 | tf_op jit(solution)/shard_map/all_to_all | solution.py:387
  31.7 2.1 %collective-permute-start.3 = (bf16[4,192,128]{2,1,0:T(8,128)(2,1)S(1)}, bf16[4,192,128]{2,1,0:T(8,128)(2,1)S(1)}, u32[]{:S(2)}, u32[]{:S(2)}) collective-permute-start(bf16[4,192,128]{2,1,0:T(8,128)(2,1)S(1)} %slice.17), channel_id=1, source_target_pairs={{0,64},{64,128},{128,192},{192,0},{1,65},{65,129},{129,193},{193,1... | collective-permute-start | bytes 589832 | tf_op jit(solution)/shard_map/ppermute | solution.py:393
  33.8 2.3 %collective-permute-start.5 = (bf16[4,192,128]{2,1,0:T(8,128)(2,1)S(1)}, bf16[4,192,128]{2,1,0:T(8,128)(2,1)S(1)}, u32[]{:S(2)}, u32[]{:S(2)}) collective-permute-start(bf16[4,192,128]{2,1,0:T(8,128)(2,1)S(1)} %slice.17), channel_id=1, source_target_pairs={{0,192},{64,0},{128,64},{192,128},{1,193},{65,1},{129,65},{193,129... | collective-permute-start | bytes 589832 | tf_op jit(solution)/shard_map/ppermute | solution.py:394
  36.1 1.3 %collective-permute-start = (bf16[4,96,128]{2,1,0:T(8,128)(2,1)S(1)}, bf16[4,96,128]{2,1,0:T(8,128)(2,1)S(1)}, u32[]{:S(2)}, u32[]{:S(2)}) collective-permute-start(bf16[4,96,128]{2,1,0:T(8,128)(2,1)S(1)} %slice.16), channel_id=1, source_target_pairs={{0,4},{4,0},{8,12},{12,8},{1,5},{5,1},{9,13},{13,9},{2,6},{6,2},{1... | collective-permute-start | bytes 294920 | tf_op jit(solution)/shard_map/ppermute | solution.py:390
  37.4 2.5 %collective-permute-start.1 = (bf16[4,96,128]{2,1,0:T(8,128)(2,1)S(1)}, bf16[4,96,128]{2,1,0:T(8,128)(2,1)S(1)}, u32[]{:S(2)}, u32[]{:S(2)}) collective-permute-start(bf16[4,96,128]{2,1,0:T(8,128)(2,1)S(1)} %slice.16), channel_id=1, source_target_pairs={{0,8},{4,12},{8,0},{12,4},{1,9},{5,13},{9,1},{13,5},{2,10},{6,14},... | collective-permute-start | bytes 294920 | tf_op jit(solution)/shard_map/ppermute | solution.py:390
  39.9 0.2 collective-permute-start.2
  40.1 0.0 collective-permute-done.q1_ref
  40.1 0.0 copy-done.3
  40.1 2.6 %collective-permute-start.7 = (bf16[256,1024]{1,0:T(8,128)(2,1)S(1)}, bf16[256,1024]{1,0:T(8,128)(2,1)}, u32[]{:S(2)}, u32[]{:S(2)}) collective-permute-start(bf16[256,1024]{1,0:T(8,128)(2,1)S(1)} %copy-done.3), channel_id=1, source_target_pairs={{0,2},{2,0},{1,3},{3,1},{4,6},{6,4},{5,7},{7,5},{8,10},{10,8},{9,1... | collective-permute-start | bytes 1572872 | tf_op jit(solution)/shard_map/ppermute | solution.py:350
  42.7 0.3 collective-permute-done.1.q2_ref
  42.9 2.8 %collective-permute-done.2.q3_ref = bf16[4,96,128]{2,1,0:T(8,128)(2,1)S(1)} collective-permute-done((bf16[4,96,128]{2,1,0:T(8,128)(2,1)S(1)}, bf16[4,96,128]{2,1,0:T(8,128)(2,1)S(1)}, u32[]{:S(2)}, u32[]{:S(2)}) %collective-permute-start.2) | collective-permute-done | bytes 98336 | tf_op jit(solution)/shard_map/ppermute | solution.py:390
  45.7 3.6 %attend_first.1 = (bf16[3072,128]{1,0:T(8,128)(2,1)S(1)}, f32[2,3072,128]{2,1,0:T(8,128)S(1)}) custom-call(bf16[4,288,128]{2,1,0:T(8,128)(2,1)S(1)} %all_to_all.10.own_ref, bf16[4,96,128]{2,1,0:T(8,128)(2,1)S(1)} %collective-permute-done.q1_ref, bf16[4,96,128]{2,1,0:T(8,128)(2,1)S(1)} %collective-permute-done.1.q2_ref, ...), custom_call_target="tpu_custom_call" | custom-call | flops 603979776 | bytes 3932160 | tf_op jit(solution)/shard_map/attend_first/pallas_call | solution.py:403
  49.3 0.0 collective-permute-done.3.kv1_ref
  49.3 1.3 %collective-permute-start.4 = (bf16[2,192,128]{2,1,0:T(8,128)(2,1)S(1)}, bf16[2,192,128]{2,1,0:T(8,128)(2,1)S(1)}, u32[]{:S(2)}, u32[]{:S(2)}) collective-permute-start(bf16[2,192,128]{2,1,0:T(8,128)(2,1)S(1)} %slice.18), channel_id=1, source_target_pairs={{0,64},{64,128},{128,192},{192,0},{1,65},{65,129},{129,193},{193,1... | collective-permute-start | bytes 294920 | tf_op jit(solution)/shard_map/ppermute | solution.py:395
  50.7 0.0 collective-permute-done.5.kv2_ref
  50.7 2.4 %collective-permute-start.6 = (bf16[2,192,128]{2,1,0:T(8,128)(2,1)S(1)}, bf16[2,192,128]{2,1,0:T(8,128)(2,1)S(1)}, u32[]{:S(2)}, u32[]{:S(2)}) collective-permute-start(bf16[2,192,128]{2,1,0:T(8,128)(2,1)S(1)} %slice.19), channel_id=1, source_target_pairs={{0,192},{64,0},{128,64},{192,128},{1,193},{65,1},{129,65},{193,129... | collective-permute-start | bytes 294920 | tf_op jit(solution)/shard_map/ppermute | solution.py:396
  53.1 6.8 %attend_next.1.before_ref = f32[2,3072,128]{2,1,0:T(8,128)S(1)} custom-call(bf16[3072,128]{1,0:T(8,128)(2,1)S(1)} %get-tuple-element.10.queries_ref, bf16[4,192,128]{2,1,0:T(8,128)(2,1)S(1)} %collective-permute-done.3.kv1_ref, bf16[4,192,128]{2,1,0:T(8,128)(2,1)S(1)} %collective-permute-done.5.kv2_ref, f32[2,3072,128]{2,1,0:T(8,128)S(1)} %get-tuple-element.11.before_ref), custom_call_target="tpu_custom_call" | custom-call | flops 1207959552 | bytes 3932160 | tf_op jit(solution)/shard_map/attend_next/pallas_call | solution.py:415
  59.9 0.0 collective-permute-done.4.kv1_ref
  59.9 0.0 collective-permute-done.6.kv2_ref
  59.9 0.0 copy-start
  59.9 0.0 copy-start.2
  59.9 0.0 copy-start.6
  59.9 4.8 %attend_last.1 = bf16[4,4,128,128]{3,2,1,0:T(8,128)(2,1)} custom-call(s32[1]{0:T(128)} %bitcast.1.place_ref, bf16[3072,128]{1,0:T(8,128)(2,1)S(1)} %get-tuple-element.10.queries_ref, bf16[2,192,128]{2,1,0:T(8,128)(2,1)S(1)} %collective-permute-done.4.kv1_ref, bf16[2,192,128]{2,1,0:T(8,128)(2,1)S(1)} %collective-permute-done.6.kv2_ref, ...), custom_call_target="tpu_custom_call" | custom-call | flops 603979776 | bytes 3932160 | tf_op jit(solution)/shard_map/attend_last/pallas_call | solution.py:425
  64.7 0.0 copy-start.4
  64.7 0.0 copy-start.5
  64.7 8.5 %all-to-all-start.1 = ((bf16[64,32,128]{2,1,0:T(8,128)(2,1)}), bf16[64,32,128]{2,1,0:T(8,128)(2,1)S(1)}, u32[]{:S(2)}, u32[]{:S(2)}) async-start(bf16[64,32,128]{2,1,0:T(8,128)(2,1)} %bitcast.6), calls=%async_computation.1 | async-start | bytes 1048576 | tf_op jit(solution)/shard_map/all_to_all | solution.py:434
  73.2 0.5 collective-permute-start.8
  73.8 0.0 collective-permute-done.7.wo2
  73.8 0.3 collective-permute-start.9
  74.1 0.0 copy-done
  74.1 0.0 copy-done.2
  74.1 0.0 copy-done.6
  74.1 0.6 write_query.1.query_ref
  74.8 0.7 collective-permute-done.8.wo1
  75.4 1.0 %collective-permute-done.9.wo3 = bf16[256,1024]{1,0:T(8,128)(2,1)} collective-permute-done((bf16[256,1024]{1,0:T(8,128)(2,1)}, bf16[256,1024]{1,0:T(8,128)(2,1)}, u32[]{:S(2)}, u32[]{:S(2)}) %collective-permute-start.9) | collective-permute-done | bytes 524320 | tf_op jit(solution)/shard_map/ppermute | solution.py:436
  76.4 9.5 %all-to-all-done.1.got_ref = bf16[64,32,128]{2,1,0:T(8,128)(2,1)S(1)} async-done(((bf16[64,32,128]{2,1,0:T(8,128)(2,1)}), bf16[64,32,128]{2,1,0:T(8,128)(2,1)S(1)}, u32[]{:S(2)}, u32[]{:S(2)}) %all-to-all-start.1) | async-done | bytes 524320 | tf_op jit(solution)/shard_map/all_to_all | solution.py:434
  85.9 0.0 copy-done.4
  85.9 0.0 copy-done.5
  85.9 4.5 %back.1 = (bf16[768,512]{1,0:T(8,128)(2,1)}, bf16[48,1024]{1,0:T(8,128)(2,1)}) custom-call(s32[1]{0:T(128)} %bitcast.place_ref, bf16[64,32,128]{2,1,0:T(8,128)(2,1)S(1)} %all-to-all-done.1.got_ref, bf16[48,1024]{1,0:T(8,128)(2,1)S(1)} %copy-done.4, f32[1,1024]{1,0:T(1,128)S(1)} %bitcast.9, bf16[768,512]{1,0:T(8,128)(2,1)S(1)} %copy-done, ...), custom_call_target="tpu_custom_call" | custom-call | tf_op jit(solution)/shard_map/back/pallas_call | solution.py:446
  (4 shorter events, 0.0 us)
Async XLA Ops:
  0.6 21.9 %copy-start.1 = (bf16[3,1024,256]{2,1,0:T(8,128)(2,1)S(1)}, bf16[3,1024,256]{2,1,0:T(8,128)(2,1)}, u32[]{:S(2)}) copy-start(bf16[3,1024,256]{2,1,0:T(8,128)(2,1)} %w_ref.2) | copy-start | bytes 4718596
  11.5 28.6 %copy-start.3 = (bf16[256,1024]{1,0:T(8,128)(2,1)S(1)}, bf16[256,1024]{1,0:T(8,128)(2,1)}, u32[]{:S(2)}) copy-start(bf16[256,1024]{1,0:T(8,128)(2,1)} %wo0.1) | copy-start | bytes 1572868
  31.7 17.6 %collective-permute-start.3 = (bf16[4,192,128]{2,1,0:T(8,128)(2,1)S(1)}, bf16[4,192,128]{2,1,0:T(8,128)(2,1)S(1)}, u32[]{:S(2)}, u32[]{:S(2)}) collective-permute-start(bf16[4,192,128]{2,1,0:T(8,128)(2,1)S(1)} %slice.17), channel_id=1, source_target_pairs={{0,64},{64,128},{128,192},{192,0},{1,65},{65,129},{129,193},{193,1... | collective-permute-start | bytes 589832 | tf_op jit(solution)/shard_map/ppermute | solution.py:393
  33.8 16.9 %collective-permute-start.5 = (bf16[4,192,128]{2,1,0:T(8,128)(2,1)S(1)}, bf16[4,192,128]{2,1,0:T(8,128)(2,1)S(1)}, u32[]{:S(2)}, u32[]{:S(2)}) collective-permute-start(bf16[4,192,128]{2,1,0:T(8,128)(2,1)S(1)} %slice.17), channel_id=1, source_target_pairs={{0,192},{64,0},{128,64},{192,128},{1,193},{65,1},{129,65},{193,129... | collective-permute-start | bytes 589832 | tf_op jit(solution)/shard_map/ppermute | solution.py:394
  36.1 3.9 %collective-permute-start = (bf16[4,96,128]{2,1,0:T(8,128)(2,1)S(1)}, bf16[4,96,128]{2,1,0:T(8,128)(2,1)S(1)}, u32[]{:S(2)}, u32[]{:S(2)}) collective-permute-start(bf16[4,96,128]{2,1,0:T(8,128)(2,1)S(1)} %slice.16), channel_id=1, source_target_pairs={{0,4},{4,0},{8,12},{12,8},{1,5},{5,1},{9,13},{13,9},{2,6},{6,2},{1... | collective-permute-start | bytes 294920 | tf_op jit(solution)/shard_map/ppermute | solution.py:390
  37.4 5.5 %collective-permute-start.1 = (bf16[4,96,128]{2,1,0:T(8,128)(2,1)S(1)}, bf16[4,96,128]{2,1,0:T(8,128)(2,1)S(1)}, u32[]{:S(2)}, u32[]{:S(2)}) collective-permute-start(bf16[4,96,128]{2,1,0:T(8,128)(2,1)S(1)} %slice.16), channel_id=1, source_target_pairs={{0,8},{4,12},{8,0},{12,4},{1,9},{5,13},{9,1},{13,5},{2,10},{6,14},... | collective-permute-start | bytes 294920 | tf_op jit(solution)/shard_map/ppermute | solution.py:390
  39.9 5.9 %collective-permute-start.2 = (bf16[4,96,128]{2,1,0:T(8,128)(2,1)S(1)}, bf16[4,96,128]{2,1,0:T(8,128)(2,1)S(1)}, u32[]{:S(2)}, u32[]{:S(2)}) collective-permute-start(bf16[4,96,128]{2,1,0:T(8,128)(2,1)S(1)} %slice.16), channel_id=1, source_target_pairs={{0,12},{4,8},{8,4},{12,0},{1,13},{5,9},{9,5},{13,1},{2,14},{6,10},... | collective-permute-start | bytes 294920 | tf_op jit(solution)/shard_map/ppermute | solution.py:390
  40.1 33.7 %collective-permute-start.7 = (bf16[256,1024]{1,0:T(8,128)(2,1)S(1)}, bf16[256,1024]{1,0:T(8,128)(2,1)}, u32[]{:S(2)}, u32[]{:S(2)}) collective-permute-start(bf16[256,1024]{1,0:T(8,128)(2,1)S(1)} %copy-done.3), channel_id=1, source_target_pairs={{0,2},{2,0},{1,3},{3,1},{4,6},{6,4},{5,7},{7,5},{8,10},{10,8},{9,1... | collective-permute-start | bytes 1572872 | tf_op jit(solution)/shard_map/ppermute | solution.py:350
  49.3 10.5 %collective-permute-start.4 = (bf16[2,192,128]{2,1,0:T(8,128)(2,1)S(1)}, bf16[2,192,128]{2,1,0:T(8,128)(2,1)S(1)}, u32[]{:S(2)}, u32[]{:S(2)}) collective-permute-start(bf16[2,192,128]{2,1,0:T(8,128)(2,1)S(1)} %slice.18), channel_id=1, source_target_pairs={{0,64},{64,128},{128,192},{192,0},{1,65},{65,129},{129,193},{193,1... | collective-permute-start | bytes 294920 | tf_op jit(solution)/shard_map/ppermute | solution.py:395
  50.7 9.2 %collective-permute-start.6 = (bf16[2,192,128]{2,1,0:T(8,128)(2,1)S(1)}, bf16[2,192,128]{2,1,0:T(8,128)(2,1)S(1)}, u32[]{:S(2)}, u32[]{:S(2)}) collective-permute-start(bf16[2,192,128]{2,1,0:T(8,128)(2,1)S(1)} %slice.19), channel_id=1, source_target_pairs={{0,192},{64,0},{128,64},{192,128},{1,193},{65,1},{129,65},{193,129... | collective-permute-start | bytes 294920 | tf_op jit(solution)/shard_map/ppermute | solution.py:396
  59.9 14.2 %copy-start = (bf16[768,512]{1,0:T(8,128)(2,1)S(1)}, bf16[768,512]{1,0:T(8,128)(2,1)}, u32[]{:S(2)}) copy-start(bf16[768,512]{1,0:T(8,128)(2,1)} %get-tuple-element.14.mid_ref) | copy-start | bytes 2359300
  59.9 14.2 %copy-start.2 = (bf16[512,512]{1,0:T(8,128)(2,1)S(1)}, bf16[512,512]{1,0:T(8,128)(2,1)}, u32[]{:S(2)}) copy-start(bf16[512,512]{1,0:T(8,128)(2,1)} %w_ref.3) | copy-start | bytes 1572868
  59.9 14.2 %copy-start.6 = (f32[512]{0:T(512)S(1)}, f32[512]{0:T(512)}, u32[]{:S(2)}) copy-start(f32[512]{0:T(512)} %param.28) | copy-start | bytes 6148
  64.7 21.2 %copy-start.4 = (bf16[48,1024]{1,0:T(8,128)(2,1)S(1)}, bf16[48,1024]{1,0:T(8,128)(2,1)}, u32[]{:S(2)}) copy-start(bf16[48,1024]{1,0:T(8,128)(2,1)} %get-tuple-element.12.latmid_ref) | copy-start | bytes 294916
  64.7 21.2 %copy-start.5 = (f32[1024]{0:T(1024)S(1)}, f32[1024]{0:T(1024)}, u32[]{:S(2)}) copy-start(f32[1024]{0:T(1024)} %param.30) | copy-start | bytes 12292
  64.7 21.2 %all-to-all-start.1 = ((bf16[64,32,128]{2,1,0:T(8,128)(2,1)}), bf16[64,32,128]{2,1,0:T(8,128)(2,1)S(1)}, u32[]{:S(2)}, u32[]{:S(2)}) async-start(bf16[64,32,128]{2,1,0:T(8,128)(2,1)} %bitcast.6), calls=%async_computation.1 | async-start | bytes 1048576 | tf_op jit(solution)/shard_map/all_to_all | solution.py:434
  73.2 2.2 %collective-permute-start.8 = (bf16[256,1024]{1,0:T(8,128)(2,1)S(1)}, bf16[256,1024]{1,0:T(8,128)(2,1)}, u32[]{:S(2)}, u32[]{:S(2)}) collective-permute-start(bf16[256,1024]{1,0:T(8,128)(2,1)S(1)} %copy-done.3), channel_id=1, source_target_pairs={{0,1},{1,0},{2,3},{3,2},{4,5},{5,4},{6,7},{7,6},{8,9},{9,8},{10,11... | collective-permute-start | bytes 1572872 | tf_op jit(solution)/shard_map/ppermute | solution.py:349
  73.8 2.6 %collective-permute-start.9 = (bf16[256,1024]{1,0:T(8,128)(2,1)}, bf16[256,1024]{1,0:T(8,128)(2,1)}, u32[]{:S(2)}, u32[]{:S(2)}) collective-permute-start(bf16[256,1024]{1,0:T(8,128)(2,1)} %collective-permute-done.7.wo2), channel_id=1, source_target_pairs={{0,1},{1,0},{2,3},{3,2},{4,5},{5,4},{6,7},{7,6},{8,9},{9,8},{10,11... | collective-permute-start | bytes 1572872 | tf_op jit(solution)/shard_map/ppermute | solution.py:436
